TPU v7x, 512 devices: a whole 4x8x8 slice. The times are simulated.
512 devices in a mesh: line: 8 (over z), cable: 8 (over y), gate: 8 (over x, core).
Axes of the slice: x: 4, y: 8, z: 8, core: 2. Of those that a mesh axis runs over, the one named last changes fastest.
Arguments:
- recorded: bfloat16 [131072, 512], P(('cable', 'gate')), may hold values from -0.5 to 0.5
- trace_order: int32 [131072], replicated, may hold values from 0 to 131071, as said below
- shot_traces: bfloat16 [32, 128, 512], P('line', 'gate'), may hold values from -0.5 to 0.5
- line_picks: int32 [32, 128], P('line', 'gate'), may hold values from 0 to 2, as said below
- aperture_mask: int32 [1024, 128], P('cable', 'gate'), may hold values 0 or 1
Outputs:
- predicted: bfloat16 [512, 32, 1024], P('gate', 'line', 'cable')
Inputs may be any that keep to these rules, and one draw needn't show every extreme that they name: `trace_order`: A permutation of 0 .. 131071; entry i names aperture point x and receiver r as x * 1024 + r. The owner of (x, r) is the device of cable r // 128 and gate x // 16. The 2048 entries of one aligned block of the list (those of one cable and gate device) name 64, 32 or 16 pairs of each owner, never more than 64, and exactly 64 for some owners. `line_picks`: value v at shot slot j of sail line l takes the shot of slot j on line l + v - 1; v is never 0 on the first line nor 2 on the last.
All inputs are finite; a program needn't handle non-finite values. No bound on the sum of `aperture_mask` on one device may be relied on, other than what follows from the above.
Results may differ from a plain program's by a relative error of at most 0.001.
Values may be sent and summed in bfloat16 or wider, within the bound.
No kernel may reach another device: no remote copies, remote signals or barrier semaphores. Data moves between devices by JAX's collectives and lax.ppermute only.
A program may use at most 64 MiB of HBM per device.

v0:
```python
import math

import jax
import jax.numpy as jnp
from jax import lax
from jax.sharding import PartitionSpec as P

REC_DEV = 128
APT_DEV = 16


def padded_2(block, sides, width):
    for axis, dim in sides:
        count = lax.axis_size(axis)
        forward = [(i, i + 1) for i in range(count - 1)]
        backward = [(target, source) for source, target in forward]
        low = lax.ppermute(
            lax.slice_in_dim(block, block.shape[dim] - width, None, axis=dim), axis, forward
        )
        high = lax.ppermute(lax.slice_in_dim(block, 0, width, axis=dim), axis, backward)
        block = jnp.concatenate([low, block, high], axis=dim)
    return block


def toeplitz_blocks(near_traces, block_width):
    shot_count, point_count, sample_count = near_traces.shape
    lag_count = sample_count // block_width
    window_len = 2 * block_width
    padded = jnp.concatenate(
        [jnp.zeros((shot_count, point_count, block_width), near_traces.dtype), near_traces], axis=2
    )
    pieces = padded.reshape(shot_count, point_count, lag_count + 1, block_width)
    windows = jnp.concatenate([pieces[:, :, :lag_count], pieces[:, :, 1:]], axis=3)
    windows = jnp.flip(windows, axis=3)
    flat_len = shot_count * point_count * window_len
    windows = jnp.transpose(windows, (2, 0, 1, 3)).reshape(lag_count, flat_len)

    def one_lag(flat_window):
        tiled_rows = jnp.tile(flat_window, block_width)[: block_width * (flat_len - 1)]
        tiled_rows = tiled_rows.reshape(block_width, flat_len - 1)
        tiled_rows = jnp.pad(tiled_rows, ((0, 0), (0, 1)))
        tiled_rows = tiled_rows.reshape(block_width, shot_count, point_count, window_len)
        tiled_rows = tiled_rows[:, :, :, block_width - 1 : window_len - 1]
        return tiled_rows.reshape(block_width * shot_count, point_count * block_width)

    return lax.map(one_lag, windows)


def owner_of(flat_index, receivers, gate_count):
    aperture = flat_index // receivers
    receiver = flat_index % receivers
    owner_dev = receiver // REC_DEV * gate_count + aperture // APT_DEV
    local_row = receiver % REC_DEV * APT_DEV + aperture % APT_DEV
    return (owner_dev, local_row)


def regroup(traces, trace_order, aperture_mask, block_width):
    owner_count = lax.axis_size(("cable", "gate"))
    gate_count = lax.axis_size("gate")
    my_owner = lax.axis_index(("cable", "gate"))
    per_device = traces.shape[0]
    sample_width = traces.shape[1]
    capacity = 2 * per_device // owner_count
    receivers = REC_DEV * lax.axis_size("cable")
    my_orders = lax.dynamic_slice_in_dim(trace_order, my_owner * per_device, per_device)
    send_owner = owner_of(my_orders, receivers, gate_count)[0]
    onehot_send = (send_owner[:, None] == jnp.arange(owner_count, dtype=jnp.int32)[None, :]).astype(
        jnp.int32
    )
    earlier = jnp.cumsum(onehot_send, axis=0) - onehot_send
    send_rank = jnp.sum(earlier * onehot_send, axis=1)
    send_slot = send_owner * capacity + send_rank
    outgoing = (
        jnp.zeros((owner_count * capacity, sample_width), traces.dtype).at[send_slot].set(traces)
    )
    outgoing = outgoing.reshape(owner_count, capacity * sample_width)
    incoming = lax.all_to_all(outgoing, ("cable", "gate"), split_axis=0, concat_axis=0, tiled=True)
    incoming = incoming.reshape(owner_count * capacity, sample_width)
    all_orders = trace_order.reshape(owner_count, per_device)
    all_owner, all_rows = owner_of(all_orders, receivers, gate_count)
    arrives = (all_owner == my_owner).astype(jnp.int32)
    arrive_rank = jnp.cumsum(arrives, axis=1) - arrives
    source_base = jnp.arange(owner_count, dtype=jnp.int32)[:, None] * capacity
    target_slot = jnp.where(arrives == 1, source_base + arrive_rank, owner_count * capacity)
    slot_rows = jnp.full((owner_count * capacity,), per_device, jnp.int32)
    slot_rows = slot_rows.at[target_slot.reshape(-1)].set(all_rows.reshape(-1), mode="drop")
    gathers = (
        jnp.zeros((per_device, sample_width), traces.dtype).at[slot_rows].set(incoming, mode="drop")
    )
    weights = aperture_mask.astype(traces.dtype)[:, :, None]
    gathers = gathers.reshape(REC_DEV, APT_DEV, sample_width) * weights
    gathers = gathers.reshape(REC_DEV, APT_DEV, sample_width // block_width, block_width)
    return jnp.transpose(gathers, (2, 0, 1, 3)).reshape(
        sample_width // block_width, REC_DEV, APT_DEV * block_width
    )


def on_device(recorded, trace_order, shot_traces, line_picks, aperture_mask):
    sample_count = recorded.shape[1]
    gate_count = lax.axis_size("gate")
    line_count = lax.axis_size("line")
    block_width = math.gcd(64, math.gcd(sample_count // gate_count, sample_count // line_count))
    gather_blocks = regroup(recorded, trace_order, aperture_mask, block_width)
    shot_block = shot_traces.shape[0]
    beside = padded_2(shot_traces, (("line", 0),), shot_block)
    pick_code = line_picks[:, :, None]
    near_traces = jnp.where(
        pick_code == 0,
        beside[:shot_block],
        jnp.where(pick_code == 1, beside[shot_block : 2 * shot_block], beside[2 * shot_block :]),
    )
    toeplitz = toeplitz_blocks(near_traces, block_width)
    receiver_count = gather_blocks.shape[1]
    row_start = jnp.int32(0)
    pieces = []
    for offset in range(lax.axis_size("gate") * (sample_count // gate_count) // block_width):
        out_block = row_start // block_width + offset

        def add_lag(earlier, running):
            lagged = lax.dynamic_index_in_dim(toeplitz, out_block - earlier, 0, False)
            source = lax.dynamic_index_in_dim(gather_blocks, earlier, 0, False)
            return running + lax.dot_general(
                lagged, source, (((1,), (1,)), ((), ())), preferred_element_type=jnp.float32
            )

        running = lax.fori_loop(
            0,
            out_block + 1,
            add_lag,
            jnp.zeros((block_width * shot_block, receiver_count), jnp.float32),
        )
        pieces.append(running.reshape(block_width, shot_block, receiver_count))
    summed = lax.psum_scatter(
        jnp.concatenate(pieces, axis=0), "gate", scatter_dimension=0, tiled=True
    )
    return summed.astype(jnp.bfloat16)


def solution(mesh):
    placed = (
        P(("cable", "gate"), None),
        P(),
        P("line", "gate", None),
        P("line", "gate"),
        P("cable", "gate"),
    )
    return jax.shard_map(
        on_device, mesh=mesh, in_specs=placed, out_specs=P("gate", "line", "cable"), check_vma=False
    )
```

profile of v0, /device:TPU:1, one launch (start us, length us, event | category | flops | bytes accessed | tf_op | source)
XLA Modules:
  0.0 838.5 jit_solution(14942572538178996334)
XLA Ops:
  0.0 5.0 collective-permute-start
  7.8 18.1 %reduce-window.16 = s32[64,16,128]{2,1,0:T(8,128)S(1)} reduce-window(s32[64,16,128]{2,1,0:T(8,128)S(1)} %fusion.63, s32[]{:T(128)} %constant.419.clone.1), window={size=1x1x128 pad=0_0x0_0x127_0}, to_apply=%region_5.6 | reduce-window | flops 16646144 | bytes 1048580 | tf_op jit(solution)/shard_map/reduce-window.2
  27.3 12.6 %scatter_custom_fusion.1 = bf16[4096,512]{1,0:T(8,128)(2,1)} fusion(s32[2048]{0:T(1024)S(1)} %compare_select_fusion.2, bf16[2048,512]{1,0:T(8,128)(2,1)} %param.21, bf16[]{:T(256)} %constant.420.clone.1), kind=kCustom, calls=%fused_computation.50 | custom fusion | bytes 4194816 | tf_op jit(solution)/shard_map/scatter | solution.py:74
  39.9 19.1 %all_to_all.8 = bf16[64,1,32768]{2,1,0:T(2,128)(2,1)} reshape(bf16[4096,512]{1,0:T(8,128)(2,1)} %scatter_custom_fusion.1) | data formatting | bytes 8388608 | tf_op jit(solution)/shard_map/all_to_all | solution.py:77
  59.5 26.7 %reduce.3 = bf16[64,32768]{1,0:T(8,128)(2,1)} reduce(bf16[64,1,32768]{2,1,0:T(2,128)(2,1)} %all_to_all.8, bf16[]{:T(256)} %broadcast.226), dimensions={1}, to_apply=%all_to_all.8.reduce_sub_computation | reduce | bytes 8388610 | tf_op jit(solution)/shard_map/all_to_all | solution.py:77
  86.2 7.8 reshape.184
  94.0 11.3 %all-to-all-start = ((bf16[64,2,16384]{2,1,0:T(2,128)(2,1)}), bf16[64,2,16384]{2,1,0:T(2,128)(2,1)}, u32[]{:S(2)}, u32[]{:S(2)}) async-start(bf16[64,2,16384]{2,1,0:T(2,128)(2,1)} %reshape.184), calls=%async_computation | async-start | bytes 8388608 | tf_op jit(solution)/shard_map/all_to_all | solution.py:77
  106.7 18.1 %reduce-window.14 = s32[64,16,128]{2,1,0:T(8,128)S(1)} reduce-window(s32[64,16,128]{2,1,0:T(8,128)S(1)} %fusion.65, s32[]{:T(128)} %constant.419.clone.1), window={size=1x1x128 pad=0_0x0_0x127_0}, to_apply=%region_2.3 | reduce-window | flops 16646144 | bytes 1048580 | tf_op jit(solution)/shard_map/reduce-window
  125.8 1.5 fusion.50
  127.4 478.4 %scatter_custom_fusion = s32[4096]{0:T(1024)S(1)} fusion(s32[131072]{0:T(1024)S(1)} %get-tuple-element.768, s32[131072]{0:T(1024)S(1)} %get-tuple-element.767, s32[]{:T(128)} %constant.422.clone.1), kind=kCustom, calls=%fused_computation.160 | custom fusion | bytes 16388 | tf_op jit(solution)/shard_map/scatter | solution.py:86
  608.6 34.0 %while.108 = (s32[]{:T(128)}, bf16[8,256,1024]{2,1,0:T(8,128)(2,1)}, bf16[8,8192]{1,0:T(8,128)(2,1)S(1)}, s32[]{:T(128)}) while((s32[]{:T(128)}, bf16[8,256,1024]{2,1,0:T(8,128)(2,1)}, bf16[8,8192]{1,0:T(8,128)(2,1)S(1)}, s32[]{:T(128)}) %tuple.262), condition=%wide.region_1.2_spmd, body=%wide.region_0.1_spmd.sunk | while | flops 2 | bytes 12631749 | solution.py:46
  609.1 1.4 reshape.187
  613.4 1.4 reshape.187
  617.7 1.4 reshape.187
  621.9 1.4 reshape.187
  626.1 1.4 reshape.187
  630.4 1.4 reshape.187
  634.6 1.4 reshape.187
  638.9 1.4 reshape.187
  642.6 19.8 %reshape.185 = bf16[64,1,32768]{2,1,0:T(2,128)(2,1)} reshape(bf16[64,2,16384]{2,1,0:T(2,128)(2,1)} %all-to-all-done) | data formatting | bytes 8388608
  662.4 26.1 %reduce.1 = bf16[64,32768]{1,0:T(8,128)(2,1)} reduce(bf16[64,1,32768]{2,1,0:T(2,128)(2,1)} %reshape.185, bf16[]{:T(256)} %constant.451), dimensions={1}, to_apply=%all_to_all.7.reduce_sub_computation | reduce | bytes 8388610 | tf_op jit(solution)/shard_map/all_to_all | solution.py:77
  688.4 7.4 reshape.168
  695.9 19.5 %scatter_custom_fusion.2 = bf16[2048,512]{1,0:T(8,128)(2,1)S(1)} fusion(s32[4096]{0:T(1024)S(1)} %compare_select_fusion.1, bf16[4096,512]{1,0:T(8,128)(2,1)} %reshape.168, bf16[]{:T(256)} %constant.420.clone.1), kind=kCustom, calls=%fused_computation.53 | custom fusion | bytes 2097664 | tf_op jit(solution)/shard_map/scatter | solution.py:88
  715.3 3.7 reshape.138
  719.0 5.0 multiply_bitcast_fusion
  724.0 1.9 copy-done
  726.7 5.5 copy.43
  735.0 2.7 while.109
  737.8 4.1 while.110
  740.5 1.3 convolution_add_fusion.15
  741.9 5.5 while.111
  741.9 1.3 convolution_add_fusion.16
  743.3 1.3 convolution_add_fusion.16
  744.6 1.3 convolution_add_fusion.16
  746.0 1.3 convolution_add_fusion.16
  747.4 6.8 while.112
  747.4 1.3 convolution_add_fusion.17
  748.7 1.3 convolution_add_fusion.17
  751.5 1.3 convolution_add_fusion.17
  754.2 8.2 while.113
  762.4 9.5 %while.114 = (s32[]{:T(128)}, f32[256,128]{1,0:T(8,128)S(1)}, bf16[8,256,1024]{2,1,0:T(8,128)(2,1)}, bf16[8,128,1024]{1,2,0:T(8,128)(2,1)S(1)}, s32[]{:T(128)}, /*index=5*/s32[]{:T(128)}, s32[]{:T(128)}, s32[]{:T(128)}) while((s32[]{:T(128)}, f32[256,128]{1,0:T(8,128)S(1)}, bf16[8,256,1024]{2,1,0:T(8,128)(2,1)}, ...), condition=%wide.region_21.22_spmd, body=%wide.region_20.21_spmd.sunk | while | flops 67141640 | bytes 1048723 | solution.py:126
  763.8 1.3 convolution_add_fusion.19
  766.5 1.3 convolution_add_fusion.19
  769.3 1.3 convolution_add_fusion.19
  772.0 10.9 %while.115 = (s32[]{:T(128)}, f32[256,128]{1,0:T(8,128)S(1)}, bf16[8,256,1024]{2,1,0:T(8,128)(2,1)}, bf16[8,128,1024]{1,2,0:T(8,128)(2,1)S(1)}, s32[]{:T(128)}, /*index=5*/s32[]{:T(128)}, s32[]{:T(128)}, s32[]{:T(128)}) while((s32[]{:T(128)}, f32[256,128]{1,0:T(8,128)S(1)}, bf16[8,256,1024]{2,1,0:T(8,128)(2,1)}, ...), condition=%wide.region_23.24_spmd, body=%wide.region_22.23_spmd.sunk | while | flops 67141640 | bytes 1048723 | solution.py:126
  778.8 1.3 convolution_add_fusion.20
  781.6 1.3 convolution_add_fusion.20
  787.5 50.3 %all-reduce.4 = bf16[512,4,128]{2,1,0:T(4,128)(2,1)S(1)} all-reduce(f32[512,4,128]{2,1,0:T(4,128)} %constant_dynamic-update-slice_fusion.1), channel_id=2, replica_groups=mesh['line'=8,'cable'=8,'gate'=8] {'gate'}, use_global_device_ids=true, to_apply=%region_24.25.clone | all-reduce | flops 262144 | bytes 1572864
  (148 shorter events, 69.8 us)
Async XLA Ops:
  0.0 27.2 %copy-start.1 = (s32[131072]{0:T(1024)S(1)}, s32[131072]{0:T(1024)}, u32[]{:S(2)}) copy-start(s32[131072]{0:T(1024)} %param.22) | copy-start | bytes 1572868
  0.0 607.9 %collective-permute-start = (bf16[4,16,512]{2,1,0:T(8,128)(2,1)}, bf16[4,16,512]{2,1,0:T(8,128)(2,1)S(1)}, u32[]{:S(2)}, u32[]{:S(2)}) collective-permute-start(bf16[4,16,512]{2,1,0:T(8,128)(2,1)} %param.23), channel_id=1, source_target_pairs={{0,64},{64,128},{128,192},{192,256},{256,320},{320,384},{384,448},... | collective-permute-start | bytes 196616 | tf_op jit(solution)/shard_map/ppermute | solution.py:17
  5.0 602.9 %collective-permute-start.1 = (bf16[4,16,512]{2,1,0:T(8,128)(2,1)}, bf16[4,16,512]{2,1,0:T(8,128)(2,1)S(1)}, u32[]{:S(2)}, u32[]{:S(2)}) collective-permute-start(bf16[4,16,512]{2,1,0:T(8,128)(2,1)} %param.23), channel_id=1, source_target_pairs={{64,0},{128,64},{192,128},{256,192},{320,256},{384,320},{448,384},... | collective-permute-start | bytes 196616 | tf_op jit(solution)/shard_map/ppermute | solution.py:20
  94.0 548.6 %all-to-all-start = ((bf16[64,2,16384]{2,1,0:T(2,128)(2,1)}), bf16[64,2,16384]{2,1,0:T(2,128)(2,1)}, u32[]{:S(2)}, u32[]{:S(2)}) async-start(bf16[64,2,16384]{2,1,0:T(2,128)(2,1)} %reshape.184), calls=%async_computation | async-start | bytes 8388608 | tf_op jit(solution)/shard_map/all_to_all | solution.py:77
  105.4 500.3 %copy-start.4 = (s32[4,16]{1,0:T(4,128)S(1)}, s32[4,16]{1,0:T(4,128)}, u32[]{:S(2)}) copy-start(s32[4,16]{1,0:T(4,128)} %param.24) | copy-start | bytes 772
  105.4 500.4 %copy-start.3 = (s32[128,16]{0,1:T(8,128)S(1)}, s32[128,16]{0,1:T(8,128)}, u32[]{:S(2)}) copy-start(s32[128,16]{0,1:T(8,128)} %param.25) | copy-start | bytes 24580
  105.4 502.4 %copy-start.2 = (bf16[4,16,512]{2,1,0:T(8,128)(2,1)S(1)}, bf16[4,16,512]{2,1,0:T(8,128)(2,1)}, u32[]{:S(2)}) copy-start(bf16[4,16,512]{2,1,0:T(8,128)(2,1)} %param.23) | copy-start | bytes 196612
  724.0 1.9 copy-start
where the time goes:
time: 846 us; the launch traced here: 839 us
  local copies, waits for them, and re-layouts  621 us (73%)
  other arithmetic  99.5 us (12%)
  blocking collectives  50.3 us (6%)
  matrix products  48.2 us (6%)
  starting transfers between devices  17.5 us (2%)
    scatter x1, local copies, waits for them, and re-layouts, regroup(): slot_rows.at[target_slot.reshape(-1)].set(all_rows.reshape(-1), mode='drop')  478 us
    all_to_all x2, other arithmetic, regroup(): lax.all_to_all(outgoing, ('cable', 'gate'), split_axis=0, concat_axis=0,...  52.8 us
    unnamed x1, blocking collectives  50.3 us
    dot_general x36, matrix products, add_lag(): lax.dot_general(lagged, source, (((1,), (1,)), ((), ())), preferred_eleme...  48.2 us
    another operation x6, other arithmetic  37.1 us
    unnamed x22, local copies, waits for them, and re-layouts  35.6 us
    all_to_all x2, local copies, waits for them, and re-layouts, regroup(): lax.all_to_all(outgoing, ('cable', 'gate'), split_axis=0, concat_axis=0,...  19.6 us
    scatter x1, local copies, waits for them, and re-layouts, regroup(): jnp.zeros((per_device, sample_width), traces.dtype).at[slot_rows]  19.5 us
  transfers between devices with their start and end apart: 3, of which 0 were waited for; matrix products, arithmetic and copies ran while one was open for 72% of the time, Pallas kernels for 0%

commit v1 on v0

v1 whole, which is shorter than its diff:
```python
import jax
import jax.numpy as jnp
from jax import lax
from jax.experimental import pallas as pl
from jax.experimental.pallas import tpu as pltpu
from jax.sharding import Mesh, PartitionSpec as P

NT = 512
LINES = 8
CABLES = 8
GATES = 8
CHIPS_X = 4
OWNERS = CABLES * GATES
PER_DEV = 2048
SHOT_DEV = 4
REC_DEV = 128
APT_DEV = 16
REC_BITS = 10
CAP = 64
HALF = CAP // 2
WIDTH = NT // LINES
LANES = 128
CHIPS = LINES * CHIPS_X
TAP = 16
TILE = 256

bf16 = jnp.bfloat16
f32 = jnp.float32
i32 = jnp.int32


def iota(shape, dim):
    return lax.broadcasted_iota(i32, shape, dim)


def params(**kw):
    return pltpu.CompilerParams(vmem_limit_bytes=56 * 1024 * 1024, **kw)


def owner_of(order):
    aperture = order >> REC_BITS
    receiver = order & ((1 << REC_BITS) - 1)
    return (receiver >> 7) * GATES + (aperture >> 4)


def earlier_matrix():
    return (iota((TILE, TILE), 0) < iota((TILE, TILE), 1)).astype(f32).astype(bf16)


def picked_rows(code_ref, source_ref, out_ref, finish):
    depth = source_ref.shape[0]
    rows = out_ref.shape[0]
    step = 1024

    def tile(m, carry):
        base = pl.multiple_of(m * TILE, TILE)
        total = jnp.zeros((TILE, LANES), f32)
        for c in range(depth // step):
            code = code_ref[:, c * step : (c + 1) * step] - base
            code = jnp.where((code >= 0) & (code < TILE), code, -1)
            code = code.astype(f32).astype(bf16)
            want = iota((TILE, step), 0).astype(f32).astype(bf16)
            onehot = jnp.where(want == code, bf16(1), bf16(0))
            total += jnp.dot(
                onehot, source_ref[c * step : (c + 1) * step, :], preferred_element_type=f32
            )
        out_ref[pl.ds(base, TILE), :] = finish(total, base).astype(out_ref.dtype)
        return carry

    lax.fori_loop(0, rows // TILE, tile, 0)


def send_kernel(where_ref, order_ref, rec_ref, out_ref, source, code):
    owner = owner_of(order_ref[...])
    before = earlier_matrix()
    carry = jnp.zeros((OWNERS, 1), f32)
    for c in range(PER_DEV // TILE):
        lanes = slice(c * TILE, (c + 1) * TILE)
        own = owner[:, lanes]
        onehot = jnp.where(iota((OWNERS, TILE), 0) == own, 1.0, 0.0).astype(f32)
        count = jnp.dot(onehot.astype(bf16), before, preferred_element_type=f32) + carry
        rank = jnp.sum(onehot * count, axis=0, keepdims=True).astype(i32)
        carry = carry + jnp.sum(onehot, axis=1, keepdims=True)
        slot = own * HALF + rank
        code[:, c * TILE : (c + 1) * TILE] = jnp.where(rank < HALF, slot, -1)
        code[:, PER_DEV + c * TILE : PER_DEV + (c + 1) * TILE] = jnp.where(
            rank >= HALF, slot - HALF, -1
        )
    odd = where_ref[1] == 1
    for c in range(PER_DEV // TILE):
        rows = slice(c * TILE, (c + 1) * TILE)
        here = rec_ref[rows, :].astype(f32)
        turned = pltpu.roll(here, WIDTH, 1)
        low = iota((TILE, LANES), 1) < WIDTH
        source[rows, :] = jnp.where(low, jnp.where(odd, turned, here), 0.0).astype(bf16)
        source[PER_DEV + c * TILE : PER_DEV + (c + 1) * TILE, :] = jnp.where(
            low, 0.0, jnp.where(odd, here, turned)
        ).astype(bf16)
    picked_rows(code, source, out_ref, lambda total, base: total)


def send(recorded, my_order, where):
    return pl.pallas_call(
        send_kernel,
        out_shape=jax.ShapeDtypeStruct((OWNERS * HALF, LANES), bf16),
        grid_spec=pltpu.PrefetchScalarGridSpec(
            num_scalar_prefetch=1,
            grid=(1,),
            in_specs=[
                pl.BlockSpec((1, PER_DEV), lambda i, w: (0, 0)),
                pl.BlockSpec((PER_DEV, LANES), lambda i, w: (0, w[0])),
            ],
            out_specs=pl.BlockSpec((OWNERS * HALF, LANES), lambda i, w: (0, 0)),
            scratch_shapes=[
                pltpu.VMEM((2 * PER_DEV, LANES), bf16),
                pltpu.VMEM((1, 2 * PER_DEV), i32),
            ],
        ),
        compiler_params=params(),
        name="send_rows",
    )(where, my_order, recorded)


def place_kernel(me_ref, order_ref, out_ref, key, chip_ref, row_ref):
    me = me_ref[0]
    before = earlier_matrix()
    carry = jnp.zeros((OWNERS, 1), f32)
    for c in range(PER_DEV // TILE):
        lanes = slice(c * TILE, (c + 1) * TILE)
        order = order_ref[:, lanes]
        mine = jnp.where(owner_of(order) == me, 1.0, 0.0).astype(f32)
        count = jnp.dot(mine.astype(bf16), before, preferred_element_type=f32) + carry
        carry = carry + jnp.sum(mine, axis=1, keepdims=True)
        key[:, lanes] = jnp.where(mine > 0.5, count, -1.0)
        receiver = order & (REC_DEV - 1)
        chip_ref[:, lanes] = (receiver & (CHIPS - 1)).astype(f32)
        row_ref[:, lanes] = ((receiver >> 5) * APT_DEV + ((order >> REC_BITS) & 15)).astype(f32)

    def group(g, carry):
        eight = pl.ds(pl.multiple_of(g * 8, 8), 8)
        all_keys = key[eight, :]
        chips = chip_ref[eight, :]
        local_rows = row_ref[eight, :]
        ones = jnp.ones((4, PER_DEV), f32)
        want = iota((HALF, PER_DEV), 0)
        for part in range(2):
            four = slice(4 * part, 4 * part + 4)
            values = jnp.concatenate([chips[four], local_rows[four], ones, 0 * ones], axis=0)
            values = values.astype(bf16)
            blocks = []
            for half in range(2):
                wanted = (want + half * HALF).astype(f32).astype(bf16)
                for b in range(4):
                    mine = all_keys[4 * part + b : 4 * part + b + 1].astype(bf16)
                    blocks.append(jnp.where(wanted == mine, bf16(1), bf16(0)))
            onehot = jnp.concatenate(blocks, axis=0)
            found = lax.dot_general(
                values, onehot, (((1,), (1,)), ((), ())), preferred_element_type=f32
            )
            own = (iota((16, TILE), 0) & 3) == ((iota((16, TILE), 1) & (LANES - 1)) >> 5)
            found = jnp.where(own, found, 0.0)
            chip = jnp.sum(found[0:4], axis=0, keepdims=True).astype(i32)
            row = jnp.sum(found[4:8], axis=0, keepdims=True).astype(i32)
            valid = jnp.sum(found[8:12], axis=0, keepdims=True) > 0.5
            code = chip * 32 + (row & 31)
            at = pl.ds(pl.multiple_of((2 * g + part) * LANES, LANES), LANES)
            for upper in range(2):
                placed = jnp.where(valid & ((row >> 5) == upper), code, -1)
                for half in range(2):
                    out_ref[2 * upper + half : 2 * upper + half + 1, at] = placed[
                        :, half * LANES : (half + 1) * LANES
                    ]
        return carry

    lax.fori_loop(0, OWNERS // 8, group, 0)


def place(orders, me):
    return pl.pallas_call(
        place_kernel,
        out_shape=jax.ShapeDtypeStruct((4, OWNERS * HALF), i32),
        in_specs=[
            pl.BlockSpec(memory_space=pltpu.SMEM),
            pl.BlockSpec(memory_space=pltpu.VMEM),
        ],
        out_specs=pl.BlockSpec(memory_space=pltpu.VMEM),
        scratch_shapes=[pltpu.VMEM((OWNERS, PER_DEV), f32)] * 3,
        compiler_params=params(),
        cost_estimate=pl.CostEstimate(
            flops=4 * 2**30, bytes_accessed=2**20, transcendentals=0
        ),
        name="place_rows",
    )(me, orders)


def receive_kernel(key_ref, got_ref, mask_ref, out_ref, source, code):
    for v in range(4):
        code[:, v * PER_DEV : (v + 1) * PER_DEV] = key_ref[v : v + 1, :]
    for c in range(PER_DEV // TILE):
        rows = slice(c * TILE, (c + 1) * TILE)
        here = got_ref[rows, :].astype(f32)
        turned = pltpu.roll(here, WIDTH, 1)
        low = iota((TILE, LANES), 1) < WIDTH
        parts = (
            jnp.where(low, here, 0.0),
            jnp.where(low, turned, 0.0),
            jnp.where(low, 0.0, turned),
            jnp.where(low, 0.0, here),
        )
        for v, part in enumerate(parts):
            source[v * PER_DEV + c * TILE : v * PER_DEV + (c + 1) * TILE, :] = part.astype(bf16)

    def weighted(total, base):
        return total * mask_ref[pl.ds(base, TILE), :].astype(f32)

    picked_rows(code, source, out_ref, weighted)


def receive(keys, got, weights):
    return pl.pallas_call(
        receive_kernel,
        out_shape=jax.ShapeDtypeStruct((CHIPS * 32, LANES), bf16),
        in_specs=[pl.BlockSpec(memory_space=pltpu.VMEM)] * 3,
        out_specs=pl.BlockSpec(memory_space=pltpu.VMEM),
        scratch_shapes=[
            pltpu.VMEM((4 * PER_DEV, LANES), bf16),
            pltpu.VMEM((1, 4 * PER_DEV), i32),
        ],
        compiler_params=params(),
        name="receive_rows",
    )(keys, got, weights)


def near_kernel(all_ref, near_ref):
    def one_line(line, carry):
        before = jnp.maximum(line - 1, 0)
        after = jnp.minimum(line + 1, LINES - 1)
        for gx in range(CHIPS_X):
            pick = all_ref[line, gx, 128:144, :]
            for g in range(8):
                rows = slice(g * 16, (g + 1) * 16)
                near_ref[line, rows, gx * 256 : (gx + 1) * 256] = jnp.where(
                    pick == bf16(0),
                    all_ref[before, gx, rows, :],
                    jnp.where(
                        pick == bf16(1), all_ref[line, gx, rows, :], all_ref[after, gx, rows, :]
                    ),
                )
        return carry

    lax.fori_loop(0, LINES, one_line, 0)


def near(everyone):
    return pl.pallas_call(
        near_kernel,
        out_shape=jax.ShapeDtypeStruct((LINES, 128, CHIPS_X * 256), bf16),
        in_specs=[pl.BlockSpec(memory_space=pltpu.VMEM)],
        out_specs=pl.BlockSpec(memory_space=pltpu.VMEM),
        compiler_params=params(),
        name="near_rows",
    )(everyone)


def predict_kernel(gather_ref, near_ref, out_ref, base, lagged, total):
    low = iota((APT_DEV, LANES), 1) < WIDTH
    lane = iota((TAP, LANES), 1)
    tap = iota((TAP, LANES), 0)

    def one_block(n, carry):
        gx = n // 2
        rho = n % 2
        for c in range(4):
            even = gather_ref[2 * c * CHIPS_X + gx, pl.ds(rho * 16, 16), :].astype(f32)
            odd = gather_ref[(2 * c + 1) * CHIPS_X + gx, pl.ds(rho * 16, 16), :].astype(f32)
            base[0, :, c * LANES : (c + 1) * LANES] = jnp.where(
                low, even, pltpu.roll(odd, WIDTH, 1)
            )
            base[1, :, c * LANES : (c + 1) * LANES] = jnp.where(
                low, pltpu.roll(even, WIDTH, 1), odd
            )
        for upper in range(2):
            lanes = pl.ds(pl.multiple_of((2 * upper + rho) * LANES, LANES), LANES)
            for x in range(APT_DEV):
                rows = pl.ds(pl.multiple_of((gx * APT_DEV + x) * TAP, TAP), TAP)
                last = jnp.zeros((TAP, LANES), f32)
                for c in range(4):
                    row = base[upper, x : x + 1, c * LANES : (c + 1) * LANES]
                    row = jnp.broadcast_to(row, (TAP, LANES))
                    turned = pltpu.roll(row, 0, 1, stride=1, stride_axis=0)
                    lagged[c, rows, lanes] = jnp.where(lane >= tap, turned, last).astype(bf16)
                    last = turned
        return carry

    lax.fori_loop(0, 2 * CHIPS_X, one_block, 0)

    second = iota((8, LANES), 0) >> 2
    lane8 = iota((8, LANES), 1)
    half8 = lane8 < WIDTH

    def one_line(line, carry):
        for d in range(4):
            part = jnp.dot(
                near_ref[line, 0 : 128 - 32 * d, :], lagged[d], preferred_element_type=f32
            )
            if d == 0:
                total[...] = part
            else:
                total[32 * d :, :] += part
        spill = [jnp.zeros((8, LANES), f32)] * 4
        for i in range(4):
            parts = []
            for rho in range(4):
                current = spill[rho]
                later = jnp.zeros((8, LANES), f32)
                for q in range(4):
                    rows = slice(32 * i + 8 * q, 32 * i + 8 * q + 8)
                    piece = total[rows, rho * LANES : (rho + 1) * LANES]
                    first = piece if q == 0 else pltpu.roll(piece, 32 * q, 1)
                    turned = jnp.where(
                        second == 0, first, pltpu.roll(piece, 32 * q + TAP, 1)
                    )
                    stays = lane8 >= 32 * q + TAP * second
                    current = current + jnp.where(stays, turned, 0.0)
                    later = later + jnp.where(stays, 0.0, turned)
                spill[rho] = later
                parts.append(current[0:4] + current[4:8])
            for k in range(2):
                for rho in range(2):
                    one, two = parts[rho], parts[2 + rho]
                    if k == 0:
                        packed = jnp.where(half8[0:4], one, pltpu.roll(two, WIDTH, 1))
                    else:
                        packed = jnp.where(half8[0:4], pltpu.roll(one, WIDTH, 1), two)
                    out_ref[line * GATES + 2 * i + k, 4 * rho : 4 * rho + 4, :] = packed
        return carry

    lax.fori_loop(0, LINES, one_line, 0)


def predict(gathers, near_all):
    return pl.pallas_call(
        predict_kernel,
        out_shape=jax.ShapeDtypeStruct((OWNERS, 8, LANES), f32),
        in_specs=[pl.BlockSpec(memory_space=pltpu.VMEM)] * 2,
        out_specs=pl.BlockSpec(memory_space=pltpu.VMEM),
        scratch_shapes=[
            pltpu.VMEM((2, APT_DEV, NT), f32),
            pltpu.VMEM((4, CHIPS_X * APT_DEV * TAP, 4 * LANES), bf16),
            pltpu.VMEM((128, 4 * LANES), f32),
        ],
        compiler_params=params(),
        name="predict_part",
    )(gathers, near_all)


def finish_kernel(parts_ref, out_ref):
    shots = []
    for s in range(SHOT_DEV):
        rows = []
        for rho in range(2):
            both = parts_ref[:, 0, 4 * rho + s, :] + parts_ref[:, 1, 4 * rho + s, :]
            rows.append(both)
        turned = jnp.transpose(jnp.concatenate(rows, axis=0))
        shots.append(jnp.concatenate([turned[:WIDTH], turned[WIDTH:]], axis=1))
    out_ref[...] = jnp.stack(shots, axis=1).astype(out_ref.dtype)


def finish(parts):
    return pl.pallas_call(
        finish_kernel,
        out_shape=jax.ShapeDtypeStruct((NT // GATES, SHOT_DEV, REC_DEV), bf16),
        in_specs=[pl.BlockSpec(memory_space=pltpu.VMEM)],
        out_specs=pl.BlockSpec(memory_space=pltpu.VMEM),
        compiler_params=params(),
        name="finish_sum",
    )(parts)


def on_device(recorded, trace_order, shot_traces, line_picks, aperture_mask):
    gate = ("gx", "core")
    me = lax.axis_index(("cable",) + gate).astype(i32)
    line = lax.axis_index("line").astype(i32)

    shots = shot_traces.reshape(SHOT_DEV, APT_DEV, NT // TAP, TAP)
    shots = jnp.transpose(shots, (2, 0, 1, 3)).reshape(NT // TAP * SHOT_DEV, APT_DEV * TAP)
    picks = jnp.tile(jnp.repeat(line_picks, TAP, axis=1), (4, 1)).astype(bf16)
    everyone = lax.all_gather(
        jnp.concatenate([shots, picks], axis=0), ("line", "gx"), axis=0, tiled=True
    )

    my_order = lax.dynamic_slice_in_dim(trace_order, me * PER_DEV, PER_DEV).reshape(1, PER_DEV)
    outgoing = send(recorded, my_order, jnp.stack([line // 2, line % 2]))
    got = lax.all_to_all(
        outgoing.reshape(OWNERS, HALF, LANES),
        ("cable",) + gate,
        split_axis=0,
        concat_axis=0,
        tiled=True,
    )
    keys = place(trace_order.reshape(OWNERS, PER_DEV), me.reshape(1))
    weights = aperture_mask.astype(bf16).reshape(2, 2, CHIPS, APT_DEV)
    weights = jnp.transpose(weights, (2, 1, 3, 0)).reshape(CHIPS * 32, 2)
    weights = jnp.repeat(weights, WIDTH, axis=1)
    mine = receive(keys, got.reshape(OWNERS * HALF, LANES), weights)
    gathers = lax.all_to_all(
        mine.reshape(CHIPS, 32, LANES), ("line", "gx"), split_axis=0, concat_axis=0, tiled=True
    )
    near_all = near(everyone.reshape(LINES, CHIPS_X, 144, 256))
    part = predict(gathers, near_all)
    parts = lax.all_to_all(part, ("line",) + gate, split_axis=0, concat_axis=0, tiled=True)
    return finish(parts.reshape(CHIPS, 2, 8, LANES))


def solution(mesh):
    split = Mesh(mesh.devices.reshape(LINES, CABLES, CHIPS_X, 2), ("line", "cable", "gx", "core"))
    gate = ("gx", "core")
    placed = (
        P(("cable",) + gate, None),
        P(),
        P("line", gate, None),
        P("line", gate),
        P("cable", gate),
    )
    return jax.shard_map(
        on_device,
        mesh=split,
        in_specs=placed,
        out_specs=P(gate, "line", "cable"),
        check_vma=False,
    )
```

time: 846 us -> 148 us (0.17)
  local copies, waits for them, and re-layouts: 621 us -> 6.31 us
  other arithmetic: 99.5 us -> 1.23 us
  matrix products: 48.2 us -> 0 us
  Pallas kernels: 0 us -> 41.3 us
  waiting for transfers between devices: 0.01 us -> 37 us
  blocking collectives: 50.3 us -> 24.4 us
  between operations: 1.05 us -> 13.5 us
    scatter x3 -> x0, local copies, waits for them, and re-layouts: 510 us -> none  [the longest x1 478 us: regroup(): slot_rows.at[target_slot.reshape(-1)].set(all_rows.reshape(-1), mode='drop')]
    all_to_all x2 -> x0, other arithmetic: 52.8 us -> none  [regroup(): lax.all_to_all(outgoing, ('cable', 'gate'), split_axis=0, concat_axis=0,...]
    unnamed x1 -> x0, blocking collectives: 50.3 us -> none
    dot_general x36 -> x0, matrix products: 48.2 us -> none  [add_lag(): lax.dot_general(lagged, source, (((1,), (1,)), ((), ())), preferred_eleme...]
    pallas_call x0 -> x6, Pallas kernels: none -> 41.3 us  [the longest x1 12.4 us: predict(): pl.pallas_call(predict_kernel, out_shape=jax.ShapeDtypeStruct((OWNERS, 8,...]
    another operation x6 -> x1, other arithmetic: 37.1 us -> 0.59 us  [on_device(): outgoing = send(recorded, my_order, jnp.stack([line // 2, line % 2]))]
    unnamed x22 -> x10, local copies, waits for them, and re-layouts: 35.6 us -> 1.51 us
    all_gather x0 -> x1, waiting for transfers between devices: none -> 28.9 us  [on_device(): lax.all_gather(jnp.concatenate([shots, picks], axis=0), ('line', 'gx'), a...]
  transfers between devices with their start and end apart: 3 -> 3, of which waited for: 0 -> 2; matrix products, arithmetic and copies ran while one was open for 72% -> 2% of each run, Pallas kernels for 0% -> 18%
where the time goes in v1:
time: 148 us; the launch traced here: 147 us
  Pallas kernels  41.3 us (28%)
  waiting for transfers between devices  37 us (25%)
  blocking collectives  24.4 us (16%)
  starting transfers between devices  23.7 us (16%)
  between operations  13.5 us (9%)
  local copies, waits for them, and re-layouts  6.31 us (4%)
    all_gather x1, waiting for transfers between devices, on_device(): lax.all_gather(jnp.concatenate([shots, picks], axis=0), ('line', 'gx'), a...  28.9 us
    all_to_all x1, blocking collectives, on_device(): lax.all_to_all(part, ('line',) + gate, split_axis=0, concat_axis=0, tiled...  24.4 us
    pallas_call x1, Pallas kernels, predict(): pl.pallas_call(predict_kernel, out_shape=jax.ShapeDtypeStruct((OWNERS, 8,...  12.4 us
    all_to_all x1, starting transfers between devices, on_device(): lax.all_to_all(mine.reshape(CHIPS, 32, LANES), ('line', 'gx'), split_axis...  12.1 us
    all_to_all x1, starting transfers between devices, on_device(): lax.all_to_all(outgoing.reshape(OWNERS, HALF, LANES), ('cable',) + gate,...  11.6 us
    pallas_call x1, Pallas kernels, send(): pl.pallas_call(send_kernel, out_shape=jax.ShapeDtypeStruct((OWNERS * HALF...  8.98 us
    all_to_all x1, waiting for transfers between devices, on_device(): lax.all_to_all(outgoing.reshape(OWNERS, HALF, LANES), ('cable',) + gate,...  8.1 us
    pallas_call x1, Pallas kernels, place(): pl.pallas_call(place_kernel, out_shape=jax.ShapeDtypeStruct((4, OWNERS *...  7.55 us
  transfers between devices with their start and end apart: 3, of which 2 were waited for; matrix products, arithmetic and copies ran while one was open for 2% of the time, Pallas kernels for 18%

profile of v1, /device:TPU:1, one launch (start us, length us, event | category | flops | bytes accessed | tf_op | source)
XLA Modules:
  0.0 147.4 jit_solution(10789889411228038121)
XLA Ops:
  6.5 0.0 copy-start.4
  6.5 0.0 copy-start.2
  6.5 0.0 all-gather.2.cloned.1.call-start
  6.5 1.3 reshape.54
  7.8 0.2 copy.9
  8.1 0.5 reshape.55
  8.5 0.0 copy-done.4
  8.5 0.1 broadcast_in_dim.7
  8.6 0.1 convert_element_type.16
  8.7 0.6 pad_maximum_fusion
  9.4 0.0 all-gather.2.cloned.1.call-update
  9.4 0.0 copy-done.2
  9.4 0.6 dynamic_slice.3
  10.0 0.6 pad_add_fusion.where_ref
  10.6 0.0 copy-start.3
  10.6 9.0 %send_rows.1 = bf16[2048,128]{1,0:T(8,128)(2,1)} custom-call(s32[2]{0:T(128)} %pad_add_fusion.where_ref, s32[1,2048]{1,0:T(1,128)} %bitcast.26, bf16[2048,512]{1,0:T(8,128)(2,1)} %rec_ref.1), custom_call_target="tpu_custom_call" | custom-call | tf_op jit(solution)/shard_map/send_rows/pallas_call | solution.py:103
  19.6 11.6 %all-to-all-start = ((bf16[64,32,128]{2,1,0:T(8,128)(2,1)}), bf16[64,32,128]{2,1,0:T(8,128)(2,1)S(1)}, u32[]{:S(2)}, u32[]{:S(2)}) async-start(bf16[64,32,128]{2,1,0:T(8,128)(2,1)} %bitcast.21), calls=%async_computation | async-start | bytes 1048576 | tf_op jit(solution)/shard_map/all_to_all | solution.py:394
  31.2 0.9 reshape.46.order_ref
  32.1 0.0 copy-done.3
  32.1 0.1 reshape.50
  32.2 0.1 copy.7
  32.3 0.1 reshape.51
  32.4 0.9 copy.8.mask_ref
  33.3 7.6 %place_rows.1.key_ref = s32[4,2048]{1,0:T(4,128)} custom-call(s32[1]{0:T(128)} %bitcast.me_ref, s32[64,2048]{1,0:T(8,128)} %reshape.46.order_ref), custom_call_target="tpu_custom_call" | custom-call | flops 4294967296 | bytes 1048576 | tf_op jit(solution)/shard_map/place_rows/pallas_call | solution.py:179
  40.9 8.1 %all-to-all-done = bf16[64,32,128]{2,1,0:T(8,128)(2,1)S(1)} async-done(((bf16[64,32,128]{2,1,0:T(8,128)(2,1)}), bf16[64,32,128]{2,1,0:T(8,128)(2,1)S(1)}, u32[]{:S(2)}, u32[]{:S(2)}) %all-to-all-start) | async-done | bytes 524320 | tf_op jit(solution)/shard_map/all_to_all | solution.py:394
  49.0 0.0 copy-start
  49.0 0.8 copy-done
  49.8 7.1 %receive_rows.1 = bf16[1024,128]{1,0:T(8,128)(2,1)} custom-call(s32[4,2048]{1,0:T(4,128)} %place_rows.1.key_ref, bf16[2048,128]{1,0:T(8,128)(2,1)} %bitcast.19, bf16[1024,128]{1,0:T(8,128)(2,1)} %copy.8.mask_ref), custom_call_target="tpu_custom_call" | custom-call | tf_op jit(solution)/shard_map/receive_rows/pallas_call | solution.py:220
  56.9 12.1 %all-to-all-start.1 = ((bf16[32,32,128]{2,1,0:T(8,128)(2,1)}), bf16[32,32,128]{2,1,0:T(8,128)(2,1)S(1)}, u32[]{:S(2)}, u32[]{:S(2)}) async-start(bf16[32,32,128]{2,1,0:T(8,128)(2,1)} %bitcast.24), calls=%async_computation.1 | async-start | bytes 524288 | tf_op jit(solution)/shard_map/all_to_all | solution.py:406
  69.0 28.9 %all-gather.2.cloned.1.call-done = bf16[4608,256]{1,0:T(8,128)(2,1)} async-done(((bf16[144,256]{1,0:T(8,128)(2,1)}), bf16[4608,256]{1,0:T(8,128)(2,1)}) %all-gather.2.cloned.1.call-update) | async-done | bytes 2359312 | tf_op jit(solution)/shard_map/all_gather | solution.py:388
  97.9 3.3 %near_rows.1.near_ref = bf16[8,128,1024]{2,1,0:T(8,128)(2,1)} custom-call(bf16[8,4,144,256]{3,2,1,0:T(8,128)(2,1)} %bitcast.18), custom_call_target="tpu_custom_call" | custom-call | tf_op jit(solution)/shard_map/near_rows/pallas_call | solution.py:255
  101.2 0.0 all-to-all-done.1.gather_ref
  101.2 0.0 copy-start.1
  101.2 0.7 copy-done.1
  101.9 12.4 %predict_part.1 = f32[64,8,128]{2,1,0:T(8,128)} custom-call(bf16[32,32,128]{2,1,0:T(8,128)(2,1)} %copy-done.1, bf16[8,128,1024]{2,1,0:T(8,128)(2,1)} %near_rows.1.near_ref), custom_call_target="tpu_custom_call" | custom-call | tf_op jit(solution)/shard_map/predict_part/pallas_call | solution.py:342
  114.3 24.4 %all_to_all.15 = f32[64,8,128]{2,1,0:T(8,128)} all-to-all(f32[64,8,128]{2,1,0:T(8,128)} %predict_part.1), channel_id=1, replica_groups=mesh['line'=8,'cable'=8,'gx'=4,'core'=2] {'line','gx','core'}, dimensions={0} | all-to-all | bytes 524288 | tf_op jit(solution)/shard_map/all_to_all | solution.py:411
  138.6 1.9 %finish_sum.1 = bf16[64,4,128]{2,1,0:T(4,128)(2,1)} custom-call(f32[32,2,8,128]{3,2,1,0:T(8,128)} %bitcast.22), custom_call_target="tpu_custom_call" | custom-call | tf_op jit(solution)/shard_map/finish_sum/pallas_call | solution.py:370
  (5 shorter events, 0.1 us)
Async XLA Ops:
  6.5 2.0 %copy-start.4 = (s32[4,16]{1,0:T(4,128)S(1)}, s32[4,16]{1,0:T(4,128)}, u32[]{:S(2)}) copy-start(s32[4,16]{1,0:T(4,128)} %param.8) | copy-start | bytes 772
  6.5 2.9 %copy-start.2 = (s32[131072]{0:T(1024)S(1)}, s32[131072]{0:T(1024)}, u32[]{:S(2)}) copy-start(s32[131072]{0:T(1024)} %param.6) | copy-start | bytes 1572868
  6.5 91.3 %all-gather.2.cloned.1.call-start = ((), (), s32[]{:S(2)}) async-start(), calls=%async_computation.3 | async-start | bytes 2433024 | tf_op jit(solution)/shard_map/all_gather | solution.py:388
  10.6 21.5 %copy-start.3 = (s32[128,16]{0,1:T(8,128)S(1)}, s32[128,16]{0,1:T(8,128)}, u32[]{:S(2)}) copy-start(s32[128,16]{0,1:T(8,128)} %param.9) | copy-start | bytes 24580
  19.6 29.3 %all-to-all-start = ((bf16[64,32,128]{2,1,0:T(8,128)(2,1)}), bf16[64,32,128]{2,1,0:T(8,128)(2,1)S(1)}, u32[]{:S(2)}, u32[]{:S(2)}) async-start(bf16[64,32,128]{2,1,0:T(8,128)(2,1)} %bitcast.21), calls=%async_computation | async-start | bytes 1048576 | tf_op jit(solution)/shard_map/all_to_all | solution.py:394
  49.0 0.8 copy-start
  56.9 44.3 %all-to-all-start.1 = ((bf16[32,32,128]{2,1,0:T(8,128)(2,1)}), bf16[32,32,128]{2,1,0:T(8,128)(2,1)S(1)}, u32[]{:S(2)}, u32[]{:S(2)}) async-start(bf16[32,32,128]{2,1,0:T(8,128)(2,1)} %bitcast.24), calls=%async_computation.1 | async-start | bytes 524288 | tf_op jit(solution)/shard_map/all_to_all | solution.py:406
  101.2 0.7 copy-start.1
Sparse Core Ops, SparseCore 0:
  10.5 87.3 all-gather.1

commit v2 on v1

v2 whole, which is shorter than its diff:
```python
import jax
import jax.numpy as jnp
from jax import lax
from jax.experimental import pallas as pl
from jax.experimental.pallas import tpu as pltpu
from jax.sharding import Mesh, PartitionSpec as P

NT = 512
LINES = 8
CABLES = 8
GATES = 8
CHIPS_X = 4
OWNERS = CABLES * GATES
PER_DEV = 2048
SHOT_DEV = 4
REC_DEV = 128
APT_DEV = 16
REC_BITS = 10
CAP = 64
HALF = CAP // 2
WIDTH = NT // LINES
LANES = 128
SHARES = LINES * 2
UPPER = 4
TAP = 16
TILE = 256
MOVED = 1024

bf16 = jnp.bfloat16
f32 = jnp.float32
i32 = jnp.int32


def iota(shape, dim):
    return lax.broadcasted_iota(i32, shape, dim)


def params(mib):
    return pltpu.CompilerParams(vmem_limit_bytes=mib * 1024 * 1024)


def owner_of(order):
    aperture = order >> REC_BITS
    receiver = order & ((1 << REC_BITS) - 1)
    return (receiver >> 7) * GATES + (aperture >> 4)


def earlier_matrix():
    return (iota((TILE, TILE), 0) < iota((TILE, TILE), 1)).astype(f32).astype(bf16)


def picked_rows(code_ref, source_ref, out_ref, finish):
    depth = source_ref.shape[0]
    rows = out_ref.shape[0]
    want = iota((TILE, TILE), 0).astype(f32).astype(bf16)

    def tile(m, carry):
        base = pl.multiple_of(m * MOVED, MOVED)
        total = jnp.zeros((MOVED, LANES), f32)
        for c in range(depth // TILE):
            at = slice(c * TILE, (c + 1) * TILE)
            blocks = []
            for b in range(MOVED // TILE):
                code = code_ref[:, at] - (base + b * TILE)
                code = jnp.where((code >= 0) & (code < TILE), code, -1)
                code = code.astype(f32).astype(bf16)
                blocks.append(jnp.where(want == code, bf16(1), bf16(0)))
            total += jnp.dot(
                jnp.concatenate(blocks, axis=0), source_ref[at, :], preferred_element_type=f32
            )
        out_ref[pl.ds(base, MOVED), :] = finish(total, base).astype(out_ref.dtype)
        return carry

    lax.fori_loop(0, rows // MOVED, tile, 0)


def send_kernel(where_ref, order_hbm, rec_hbm, out_ref, order_ref, rec_ref, source, code, sems):
    line, me = where_ref[0], where_ref[1]
    order_copy = pltpu.make_async_copy(
        order_hbm.at[pl.ds(pl.multiple_of(me * PER_DEV, PER_DEV), PER_DEV)], order_ref, sems.at[0]
    )
    rec_copy = pltpu.make_async_copy(
        rec_hbm.at[:, pl.ds(pl.multiple_of((line >> 1) * LANES, LANES), LANES)],
        rec_ref,
        sems.at[1],
    )
    order_copy.start()
    rec_copy.start()
    order_copy.wait()
    owner = owner_of(order_ref[...].reshape(1, PER_DEV))
    before = earlier_matrix()
    carry = jnp.zeros((OWNERS, 1), f32)
    for c in range(PER_DEV // TILE):
        lanes = slice(c * TILE, (c + 1) * TILE)
        own = owner[:, lanes]
        onehot = jnp.where(iota((OWNERS, TILE), 0) == own, 1.0, 0.0).astype(f32)
        count = jnp.dot(onehot.astype(bf16), before, preferred_element_type=f32) + carry
        rank = jnp.sum(onehot * count, axis=0, keepdims=True).astype(i32)
        carry = carry + jnp.sum(onehot, axis=1, keepdims=True)
        slot = own * HALF + rank
        code[:, c * TILE : (c + 1) * TILE] = jnp.where(rank < HALF, slot, -1)
        code[:, PER_DEV + c * TILE : PER_DEV + (c + 1) * TILE] = jnp.where(
            rank >= HALF, slot - HALF, -1
        )
    rec_copy.wait()
    odd = line & 1 == 1
    for c in range(PER_DEV // TILE):
        rows = slice(c * TILE, (c + 1) * TILE)
        here = rec_ref[rows, :].astype(f32)
        turned = pltpu.roll(here, WIDTH, 1)
        low = iota((TILE, LANES), 1) < WIDTH
        source[rows, :] = jnp.where(low, jnp.where(odd, turned, here), 0.0).astype(bf16)
        source[PER_DEV + c * TILE : PER_DEV + (c + 1) * TILE, :] = jnp.where(
            low, 0.0, jnp.where(odd, here, turned)
        ).astype(bf16)
    picked_rows(code, source, out_ref, lambda total, base: total)


def send(recorded, trace_order, where):
    return pl.pallas_call(
        send_kernel,
        out_shape=jax.ShapeDtypeStruct((OWNERS * HALF, LANES), bf16),
        in_specs=[
            pl.BlockSpec(memory_space=pltpu.SMEM),
            pl.BlockSpec(memory_space=pltpu.HBM),
            pl.BlockSpec(memory_space=pltpu.HBM),
        ],
        out_specs=pl.BlockSpec(memory_space=pltpu.VMEM),
        scratch_shapes=[
            pltpu.VMEM((PER_DEV,), i32),
            pltpu.VMEM((PER_DEV, LANES), bf16),
            pltpu.VMEM((2 * PER_DEV, LANES), bf16),
            pltpu.VMEM((1, 2 * PER_DEV), i32),
            pltpu.SemaphoreType.DMA((2,)),
        ],
        compiler_params=params(58),
        name="send_rows",
    )(where, trace_order, recorded)


def place_kernel(me_ref, order_ref, out_ref, key, chip_ref, row_ref):
    me = me_ref[0]
    before = earlier_matrix()
    carry = jnp.zeros((OWNERS, 1), f32)
    for c in range(PER_DEV // TILE):
        lanes = slice(c * TILE, (c + 1) * TILE)
        order = order_ref[:, lanes]
        mine = jnp.where(owner_of(order) == me, 1.0, 0.0).astype(f32)
        count = jnp.dot(mine.astype(bf16), before, preferred_element_type=f32) + carry
        carry = carry + jnp.sum(mine, axis=1, keepdims=True)
        key[:, lanes] = jnp.where(mine > 0.5, count, -1.0)
        receiver = order & (REC_DEV - 1)
        chip_ref[:, lanes] = (receiver & (SHARES - 1)).astype(f32)
        row_ref[:, lanes] = ((receiver >> 4) * APT_DEV + ((order >> REC_BITS) & 15)).astype(f32)

    def group(g, carry):
        eight = pl.ds(pl.multiple_of(g * 8, 8), 8)
        all_keys = key[eight, :]
        chips = chip_ref[eight, :]
        local_rows = row_ref[eight, :]
        ones = jnp.ones((4, PER_DEV), f32)
        want = iota((HALF, PER_DEV), 0)
        for part in range(2):
            four = slice(4 * part, 4 * part + 4)
            values = jnp.concatenate([chips[four], local_rows[four], ones, 0 * ones], axis=0)
            values = values.astype(bf16)
            blocks = []
            for half in range(2):
                wanted = (want + half * HALF).astype(f32).astype(bf16)
                for b in range(4):
                    mine = all_keys[4 * part + b : 4 * part + b + 1].astype(bf16)
                    blocks.append(jnp.where(wanted == mine, bf16(1), bf16(0)))
            onehot = jnp.concatenate(blocks, axis=0)
            found = lax.dot_general(
                values, onehot, (((1,), (1,)), ((), ())), preferred_element_type=f32
            )
            own = (iota((16, TILE), 0) & 3) == ((iota((16, TILE), 1) & (LANES - 1)) >> 5)
            found = jnp.where(own, found, 0.0)
            chip = jnp.sum(found[0:4], axis=0, keepdims=True).astype(i32)
            row = jnp.sum(found[4:8], axis=0, keepdims=True).astype(i32)
            valid = jnp.sum(found[8:12], axis=0, keepdims=True) > 0.5
            code = chip * 64 + (row & 63)
            at = pl.ds(pl.multiple_of((2 * g + part) * LANES, LANES), LANES)
            for upper in range(2):
                placed = jnp.where(valid & ((row >> 6) == upper), code, -1)
                for half in range(2):
                    out_ref[2 * upper + half : 2 * upper + half + 1, at] = placed[
                        :, half * LANES : (half + 1) * LANES
                    ]
        return carry

    lax.fori_loop(0, OWNERS // 8, group, 0)


def place(orders, me):
    return pl.pallas_call(
        place_kernel,
        out_shape=jax.ShapeDtypeStruct((4, OWNERS * HALF), i32),
        in_specs=[
            pl.BlockSpec(memory_space=pltpu.SMEM),
            pl.BlockSpec(memory_space=pltpu.VMEM),
        ],
        out_specs=pl.BlockSpec(memory_space=pltpu.VMEM),
        scratch_shapes=[pltpu.VMEM((OWNERS, PER_DEV), f32)] * 3,
        compiler_params=params(12),
        cost_estimate=pl.CostEstimate(
            flops=4 * 2**30, bytes_accessed=2**20, transcendentals=0
        ),
        name="place_rows",
    )(me, orders)


def receive_kernel(key_ref, got_ref, mask_ref, out_ref, source, code):
    for v in range(4):
        code[:, v * PER_DEV : (v + 1) * PER_DEV] = key_ref[v : v + 1, :]
    for c in range(PER_DEV // TILE):
        rows = slice(c * TILE, (c + 1) * TILE)
        here = got_ref[rows, :].astype(f32)
        turned = pltpu.roll(here, WIDTH, 1)
        low = iota((TILE, LANES), 1) < WIDTH
        parts = (
            jnp.where(low, here, 0.0),
            jnp.where(low, turned, 0.0),
            jnp.where(low, 0.0, turned),
            jnp.where(low, 0.0, here),
        )
        for v, part in enumerate(parts):
            source[v * PER_DEV + c * TILE : v * PER_DEV + (c + 1) * TILE, :] = part.astype(bf16)

    def weighted(total, base):
        return total * mask_ref[pl.ds(base, MOVED), :].astype(f32)

    picked_rows(code, source, out_ref, weighted)


def receive(keys, got, weights):
    return pl.pallas_call(
        receive_kernel,
        out_shape=jax.ShapeDtypeStruct((SHARES * 64, LANES), bf16),
        in_specs=[pl.BlockSpec(memory_space=pltpu.VMEM)] * 3,
        out_specs=pl.BlockSpec(memory_space=pltpu.VMEM),
        scratch_shapes=[
            pltpu.VMEM((4 * PER_DEV, LANES), bf16),
            pltpu.VMEM((1, 4 * PER_DEV), i32),
        ],
        compiler_params=params(12),
        name="receive_rows",
    )(keys, got, weights)


def near_kernel(where_ref, own_ref, other_ref, near_ref):
    me, core = where_ref[0], where_ref[1]

    def held(line):
        offset = line ^ me
        return ((offset & 1) << 2) | (offset & 2) | (offset >> 2)

    def one_line(line, carry):
        here = held(line)
        before = held(jnp.maximum(line - 1, 0))
        after = held(jnp.minimum(line + 1, LINES - 1))
        for side, all_ref in enumerate((own_ref, other_ref)):
            at = pl.multiple_of((core ^ side) * 256, 256)
            pick = all_ref[here, 128:144, :]
            first, own = pick == bf16(0), pick == bf16(1)
            for g in range(8):
                rows = slice(g * 16, (g + 1) * 16)
                near_ref[line, rows, pl.ds(at, 256)] = jnp.where(
                    first,
                    all_ref[before, rows, :],
                    jnp.where(own, all_ref[here, rows, :], all_ref[after, rows, :]),
                )
        return carry

    lax.fori_loop(0, LINES, one_line, 0)


def near(where, own, other):
    return pl.pallas_call(
        near_kernel,
        out_shape=jax.ShapeDtypeStruct((LINES, 128, 512), bf16),
        in_specs=[
            pl.BlockSpec(memory_space=pltpu.SMEM),
            pl.BlockSpec(memory_space=pltpu.VMEM),
            pl.BlockSpec(memory_space=pltpu.VMEM),
        ],
        out_specs=pl.BlockSpec(memory_space=pltpu.VMEM),
        compiler_params=params(8),
        name="near_rows",
    )(where, own, other)


def swapped(held, axis, bit):
    size = lax.axis_size(axis)
    return lax.ppermute(held, axis, [(i, i ^ bit) for i in range(size)])


def lag_rows(gather_ref, base, lagged):
    low = iota((APT_DEV, LANES), 1) < WIDTH
    lane = iota((TAP, LANES), 1)
    tap = iota((TAP, LANES), 0)

    def one_block(n, carry):
        core = n // UPPER
        rho = n % UPPER
        for c in range(4):
            rows = pl.ds(pl.multiple_of(rho * 16, 16), 16)
            even = gather_ref[4 * c + core, rows, :].astype(f32)
            odd = gather_ref[4 * c + 2 + core, rows, :].astype(f32)
            base[0, :, c * LANES : (c + 1) * LANES] = jnp.where(
                low, even, pltpu.roll(odd, WIDTH, 1)
            )
            base[1, :, c * LANES : (c + 1) * LANES] = jnp.where(
                low, pltpu.roll(even, WIDTH, 1), odd
            )
        for upper in range(2):
            lanes = pl.ds(pl.multiple_of((2 * rho + upper) * LANES, LANES), LANES)
            for x in range(APT_DEV):
                rows = pl.ds(pl.multiple_of((core * APT_DEV + x) * TAP, TAP), TAP)
                last = jnp.zeros((TAP, LANES), f32)
                for c in range(4):
                    row = base[upper, x : x + 1, c * LANES : (c + 1) * LANES]
                    row = jnp.broadcast_to(row, (TAP, LANES))
                    turned = pltpu.roll(row, 0, 1, stride=1, stride_axis=0)
                    lagged[c, rows, lanes] = jnp.where(lane >= tap, turned, last).astype(bf16)
                    last = turned
        return carry

    lax.fori_loop(0, 2 * UPPER, one_block, 0)


def sum_lines(near_ref, lagged, out_ref):
    lane = iota((8 * LINES, LANES), 1)
    low = lane < WIDTH

    for rho in range(UPPER):
        spill = [jnp.zeros((8 * LINES, LANES), f32)] * 2
        before = [jnp.zeros((8 * LINES, LANES), f32)] * 2
        for i in range(4):
            total = None
            for d in range(i + 1):
                here = near_ref[:, 32 * (i - d) : 32 * (i - d) + 32, :].reshape(32 * LINES, 512)
                part = jnp.dot(
                    here, lagged[d, :, 256 * rho : 256 * rho + 256], preferred_element_type=f32
                )
                total = part if total is None else total + part
            total = total.reshape(LINES, 4, 8, 256)
            done = []
            for upper in range(2):
                current = spill[upper]
                later = jnp.zeros((8 * LINES, LANES), f32)
                for q in range(4):
                    piece = total[:, q, :, upper * LANES : (upper + 1) * LANES]
                    piece = piece.reshape(8 * LINES, LANES)
                    if q == 0:
                        current = current + piece
                    else:
                        turned = pltpu.roll(piece, 32 * q, 1)
                        current = current + jnp.where(lane >= 32 * q, turned, 0.0)
                        later = later + jnp.where(lane >= 32 * q, 0.0, turned)
                turned = pltpu.roll(current, TAP, 1)
                moved = jnp.where(lane >= TAP, turned, before[upper])
                spill[upper] = later
                before[upper] = turned
                both = current.reshape(LINES, 8, LANES)[:, 0:4] + moved.reshape(LINES, 8, LANES)[:, 4:8]
                done.append(both.reshape(4 * LINES, LANES))
            one, two = done
            half = low[: 4 * LINES]
            rows = slice(4 * rho, 4 * rho + 4)
            even = jnp.where(half, one, pltpu.roll(two, WIDTH, 1)).reshape(LINES, 4, LANES)
            odd = jnp.where(half, pltpu.roll(one, WIDTH, 1), two).reshape(LINES, 4, LANES)
            out_ref[:, 2 * i, rows, :] = even
            out_ref[:, 2 * i + 1, rows, :] = odd


def predict_kernel(gather_ref, near_ref, out_ref, base, lagged):
    lag_rows(gather_ref, base, lagged)
    sum_lines(near_ref, lagged, out_ref)


def predict(gathers, near_all):
    return pl.pallas_call(
        predict_kernel,
        out_shape=jax.ShapeDtypeStruct((LINES, GATES, 4 * UPPER, LANES), f32),
        in_specs=[pl.BlockSpec(memory_space=pltpu.VMEM)] * 2,
        out_specs=pl.BlockSpec(memory_space=pltpu.VMEM),
        scratch_shapes=[
            pltpu.VMEM((2, APT_DEV, NT), f32),
            pltpu.VMEM((4, 2 * APT_DEV * TAP, 2 * UPPER * LANES), bf16),
        ],
        compiler_params=params(20),
        name="predict_part",
    )(gathers, near_all)


def finish_kernel(parts_ref, out_ref):
    total = jnp.sum(parts_ref[...], axis=1).reshape(SHARES, 4 * UPPER, LANES)
    shots = []
    for s in range(SHOT_DEV):
        rows = []
        for rho in range(UPPER):
            rows.append(total[:, 4 * rho + s, :])
        turned = jnp.transpose(jnp.concatenate(rows, axis=0))
        shots.append(jnp.concatenate([turned[:WIDTH], turned[WIDTH:]], axis=1))
    out_ref[...] = jnp.stack(shots, axis=1).astype(out_ref.dtype)


def finish(parts):
    return pl.pallas_call(
        finish_kernel,
        out_shape=jax.ShapeDtypeStruct((NT // GATES, SHOT_DEV, REC_DEV), bf16),
        in_specs=[pl.BlockSpec(memory_space=pltpu.VMEM)],
        out_specs=pl.BlockSpec(memory_space=pltpu.VMEM),
        compiler_params=params(6),
        name="finish_sum",
    )(parts)


def on_device(recorded, trace_order, shot_traces, line_picks, aperture_mask):
    gate = ("gx", "core")
    me = lax.axis_index(("cable",) + gate).astype(i32)
    line = lax.axis_index("line").astype(i32)

    shots = shot_traces.reshape(SHOT_DEV, APT_DEV, NT // TAP, TAP)
    shots = jnp.transpose(shots, (2, 0, 1, 3)).reshape(NT // TAP * SHOT_DEV, APT_DEV * TAP)
    picks = jnp.tile(jnp.repeat(line_picks, TAP, axis=1), (4, 1)).astype(bf16)
    held = jnp.concatenate([shots, picks], axis=0)[None]
    four = swapped(held, "line", 4)

    outgoing = send(recorded, trace_order, jnp.stack([line, me]))
    got = lax.all_to_all(
        outgoing.reshape(OWNERS, HALF, LANES),
        ("cable",) + gate,
        split_axis=0,
        concat_axis=0,
        tiled=True,
    )
    late, four, trace_order, aperture_mask = lax.optimization_barrier(
        (outgoing, four, trace_order, aperture_mask)
    )
    held = jnp.concatenate([held, four], axis=0)
    two = swapped(held, "line", 2)
    keys = place(trace_order.reshape(OWNERS, PER_DEV), me.reshape(1))
    keys, two = lax.optimization_barrier((keys, two))
    held = jnp.concatenate([held, two], axis=0)
    one = swapped(held, "line", 1)
    weights = aperture_mask.astype(bf16).reshape(2, UPPER, SHARES, APT_DEV)
    weights = jnp.transpose(weights, (2, 1, 3, 0)).reshape(SHARES * 64, 2)
    weights = jnp.repeat(weights, WIDTH, axis=1)
    mine = receive(keys, got.reshape(OWNERS * HALF, LANES), weights)
    gathers = lax.all_to_all(
        mine.reshape(SHARES, 64, LANES), ("line", "core"), split_axis=0, concat_axis=0, tiled=True
    )
    late, one = lax.optimization_barrier((mine, one))
    own = jnp.concatenate([held, one], axis=0)
    other = swapped(own, "core", 1)
    near_all = near(jnp.stack([line, lax.axis_index("core").astype(i32)]), own, other)
    part = predict(gathers, near_all)
    parts = lax.all_to_all(
        part.reshape(OWNERS, 4 * UPPER, LANES), ("line",) + gate, split_axis=0, concat_axis=0, tiled=True)
    return finish(parts.reshape(LINES, CHIPS_X, 2, 4 * UPPER, LANES))


def solution(mesh):
    split = Mesh(mesh.devices.reshape(LINES, CABLES, CHIPS_X, 2), ("line", "cable", "gx", "core"))
    gate = ("gx", "core")
    placed = (
        P(("cable",) + gate, None),
        P(),
        P("line", gate, None),
        P("line", gate),
        P("cable", gate),
    )
    return jax.shard_map(
        on_device,
        mesh=split,
        in_specs=placed,
        out_specs=P(gate, "line", "cable"),
        check_vma=False,
    )
```

time: 148 us -> 109 us (0.74)
  waiting for transfers between devices: 37 us -> 15.7 us
  starting transfers between devices: 23.7 us -> 39.9 us
  Pallas kernels: 41.3 us -> 26.3 us
  between operations: 13.5 us -> 0.21 us
  local copies, waits for them, and re-layouts: 6.31 us -> 1.85 us
    all_gather x1 -> x0, waiting for transfers between devices: 28.9 us -> none  [on_device(): lax.all_gather(jnp.concatenate([shots, picks], axis=0), ('line', 'gx'), a...]
    ppermute x0 -> x4, starting transfers between devices: none -> 21.9 us  [swapped(): return lax.ppermute(held, axis, [(i, i ^ bit) for i in range(size)])]
    pallas_call x3, Pallas kernels: 22.8 us -> 11.9 us  [the longest x1 5.66 us: predict(): pl.pallas_call(predict_kernel, out_shape=jax.ShapeDtypeStruct((LINES, GAT...]
    all_to_all x1, waiting for transfers between devices: 0.01 us -> 10.9 us  [on_device(): lax.all_to_all(mine.reshape(SHARES, 64, LANES), ('line', 'core'), split_a...]
    all_to_all x1, waiting for transfers between devices: 8.1 us -> 0.01 us  [on_device(): lax.all_to_all(outgoing.reshape(OWNERS, HALF, LANES), ('cable',) + gate,...]
    all_to_all x1, starting transfers between devices: 12.1 us -> 6.27 us  [on_device(): lax.all_to_all(mine.reshape(SHARES, 64, LANES), ('line', 'core'), split_a...]
    ppermute x0 -> x4, waiting for transfers between devices: none -> 4.87 us  [swapped(): return lax.ppermute(held, axis, [(i, i ^ bit) for i in range(size)])]
    pallas_call x1, Pallas kernels: 7.55 us -> 5.9 us  [place(): pl.pallas_call(place_kernel, out_shape=jax.ShapeDtypeStruct((4, OWNERS *...]
  transfers between devices with their start and end apart: 3 -> 6, of which waited for: 2 -> 4; matrix products, arithmetic and copies ran while one was open for 2% -> 2% of each run, Pallas kernels for 18% -> 11%
where the time goes in v2:
time: 109 us
  starting transfers between devices  39.9 us (37%)
  Pallas kernels  26.3 us (24%)
  blocking collectives  23.8 us (22%)
  waiting for transfers between devices  15.7 us (14%)
  local copies, waits for them, and re-layouts  1.85 us (2%)
    all_to_all x1, blocking collectives, on_device(): lax.all_to_all(part.reshape(OWNERS, 4 * UPPER, LANES), ('line',) + gate,...  23.8 us
    ppermute x4, starting transfers between devices, swapped(): return lax.ppermute(held, axis, [(i, i ^ bit) for i in range(size)])  21.9 us
    all_to_all x1, starting transfers between devices, on_device(): lax.all_to_all(outgoing.reshape(OWNERS, HALF, LANES), ('cable',) + gate,...  11.8 us
    all_to_all x1, waiting for transfers between devices, on_device(): lax.all_to_all(mine.reshape(SHARES, 64, LANES), ('line', 'core'), split_a...  10.9 us
    pallas_call x1, Pallas kernels, send(): pl.pallas_call(send_kernel, out_shape=jax.ShapeDtypeStruct((OWNERS * HALF...  7.61 us
    all_to_all x1, starting transfers between devices, on_device(): lax.all_to_all(mine.reshape(SHARES, 64, LANES), ('line', 'core'), split_a...  6.27 us
    pallas_call x1, Pallas kernels, place(): pl.pallas_call(place_kernel, out_shape=jax.ShapeDtypeStruct((4, OWNERS *...  5.9 us
    pallas_call x1, Pallas kernels, predict(): pl.pallas_call(predict_kernel, out_shape=jax.ShapeDtypeStruct((LINES, GAT...  5.66 us
  transfers between devices with their start and end apart: 6, of which 4 were waited for; matrix products, arithmetic and copies ran while one was open for 2% of the time, Pallas kernels for 11%

profile of v2, /device:TPU:1, one launch (start us, length us, event | category | flops | bytes accessed | tf_op | source)
XLA Modules:
  0.0 108.7 jit_solution(12699147354604102420)
XLA Ops:
  0.0 0.6 pad_add_fusion.where_ref
  0.6 0.0 copy-start.3
  0.7 0.0 copy-start.1
  0.7 7.6 %send_rows.1 = bf16[2048,128]{1,0:T(8,128)(2,1)} custom-call(s32[2]{0:T(128)} %pad_add_fusion.where_ref, s32[131072]{0:T(1024)} %order_hbm.1, bf16[2048,512]{1,0:T(8,128)(2,1)} %rec_hbm.1), custom_call_target="tpu_custom_call" | custom-call | tf_op jit(solution)/shard_map/send_rows/pallas_call | solution.py:120
  8.3 0.0 copy-start
  8.3 11.8 %all-to-all-start = ((bf16[64,32,128]{2,1,0:T(8,128)(2,1)}), bf16[64,32,128]{2,1,0:T(8,128)(2,1)S(1)}, u32[]{:S(2)}, u32[]{:S(2)}) async-start(bf16[64,32,128]{2,1,0:T(8,128)(2,1)} %bitcast.23), calls=%async_computation | async-start | bytes 1048576 | tf_op jit(solution)/shard_map/all_to_all | solution.py:431
  20.0 0.0 copy-done.3
  20.1 0.1 broadcast_in_dim.9
  20.1 0.1 convert_element_type.15
  20.3 0.0 copy-done.1
  20.3 0.4 reshape.43
  20.7 0.2 copy.7
  20.9 0.5 reshape.44
  21.4 10.6 %collective-permute-start = (bf16[1,144,256]{2,1,0:T(8,128)(2,1)S(1)}, bf16[1,144,256]{2,1,0:T(8,128)(2,1)S(1)}, u32[]{:S(2)}, u32[]{:S(2)}) collective-permute-start(bf16[1,144,256]{2,1,0:T(8,128)(2,1)S(1)} %maximum_bitcast_fusion), channel_id=1, source_target_pairs={{0,256},{64,320},{128,384},{192,448},{256,0},{320,64},{384,128},{4... | collective-permute-start | bytes 221192 | tf_op jit(solution)/shard_map/ppermute | solution.py:295
  32.0 2.2 %collective-permute-done = bf16[1,144,256]{2,1,0:T(8,128)(2,1)S(1)} collective-permute-done((bf16[1,144,256]{2,1,0:T(8,128)(2,1)S(1)}, bf16[1,144,256]{2,1,0:T(8,128)(2,1)S(1)}, u32[]{:S(2)}, u32[]{:S(2)}) %collective-permute-start) | collective-permute-done | bytes 73760 | tf_op jit(solution)/shard_map/ppermute | solution.py:295
  34.3 6.1 %collective-permute-start.1 = (bf16[2,144,256]{2,1,0:T(8,128)(2,1)S(1)}, bf16[2,144,256]{2,1,0:T(8,128)(2,1)S(1)}, u32[]{:S(2)}, u32[]{:S(2)}) collective-permute-start(bf16[2,144,256]{2,1,0:T(8,128)(2,1)S(1)} %pad_maximum_fusion.2), channel_id=1, source_target_pairs={{0,128},{64,192},{128,0},{192,64},{256,384},{320,448},{384,256},{4... | collective-permute-start | bytes 442376 | tf_op jit(solution)/shard_map/ppermute | solution.py:295
  40.4 0.0 copy-done
  40.4 0.1 reshape.45.order_ref
  40.5 0.0 copy-start.2
  40.5 5.9 %place_rows.1.key_ref = s32[4,2048]{1,0:T(4,128)S(1)} custom-call(s32[1]{0:T(128)} %bitcast.me_ref, s32[64,2048]{1,0:T(8,128)S(1)} %reshape.45.order_ref), custom_call_target="tpu_custom_call" | custom-call | flops 4294967296 | bytes 1048576 | tf_op jit(solution)/shard_map/place_rows/pallas_call | solution.py:196
  46.4 0.5 collective-permute-done.1
  47.0 1.9 %collective-permute-start.2 = (bf16[4,144,256]{2,1,0:T(8,128)(2,1)S(1)}, bf16[4,144,256]{2,1,0:T(8,128)(2,1)S(1)}, u32[]{:S(2)}, u32[]{:S(2)}) collective-permute-start(bf16[4,144,256]{2,1,0:T(8,128)(2,1)S(1)} %pad_maximum_fusion.1), channel_id=1, source_target_pairs={{0,64},{64,0},{128,192},{192,128},{256,320},{320,256},{384,448},{4... | collective-permute-start | bytes 884744 | tf_op jit(solution)/shard_map/ppermute | solution.py:295
  48.9 0.0 copy-done.2
  48.9 0.1 reshape.48
  49.0 0.1 copy.8
  49.1 0.1 reshape.49
  49.2 0.2 copy.9.mask_ref
  49.4 0.0 all-to-all-done
  49.4 5.4 %receive_rows.1 = bf16[1024,128]{1,0:T(8,128)(2,1)} custom-call(s32[4,2048]{1,0:T(4,128)S(1)} %place_rows.1.key_ref, bf16[2048,128]{1,0:T(8,128)(2,1)S(1)} %bitcast.20, bf16[1024,128]{1,0:T(8,128)(2,1)S(1)} %copy.9.mask_ref), custom_call_target="tpu_custom_call" | custom-call | tf_op jit(solution)/shard_map/receive_rows/pallas_call | solution.py:237
  54.9 2.1 %collective-permute-done.2 = bf16[4,144,256]{2,1,0:T(8,128)(2,1)S(1)} collective-permute-done((bf16[4,144,256]{2,1,0:T(8,128)(2,1)S(1)}, bf16[4,144,256]{2,1,0:T(8,128)(2,1)S(1)}, u32[]{:S(2)}, u32[]{:S(2)}) %collective-permute-start.2) | collective-permute-done | bytes 294944 | tf_op jit(solution)/shard_map/ppermute | solution.py:295
  57.0 0.1 pad_maximum_fusion.own_ref
  57.0 3.2 %collective-permute-start.3 = (bf16[8,144,256]{2,1,0:T(8,128)(2,1)S(1)}, bf16[8,144,256]{2,1,0:T(8,128)(2,1)S(1)}, u32[]{:S(2)}, u32[]{:S(2)}) collective-permute-start(bf16[8,144,256]{2,1,0:T(8,128)(2,1)S(1)} %pad_maximum_fusion.own_ref), channel_id=1, source_target_pairs={{0,1},{1,0},{2,3},{3,2},{4,5},{5,4},{6,7},{7,6},{8,9},{9,8},{10,11... | collective-permute-start | bytes 1769480 | tf_op jit(solution)/shard_map/ppermute | solution.py:295
  60.2 6.3 %all-to-all-start.1 = ((bf16[16,64,128]{2,1,0:T(8,128)(2,1)}), bf16[16,64,128]{2,1,0:T(8,128)(2,1)S(1)}, u32[]{:S(2)}, u32[]{:S(2)}) async-start(bf16[16,64,128]{2,1,0:T(8,128)(2,1)} %bitcast.8), calls=%async_computation.1 | async-start | bytes 524288 | tf_op jit(solution)/shard_map/all_to_all | solution.py:451
  66.5 0.1 pad_add_fusion.1.where_ref
  66.6 0.0 collective-permute-done.3.other_ref
  66.6 0.8 near_rows.1.near_ref
  67.4 10.9 %all-to-all-done.1.gather_ref = bf16[16,64,128]{2,1,0:T(8,128)(2,1)S(1)} async-done(((bf16[16,64,128]{2,1,0:T(8,128)(2,1)}), bf16[16,64,128]{2,1,0:T(8,128)(2,1)S(1)}, u32[]{:S(2)}, u32[]{:S(2)}) %all-to-all-start.1) | async-done | bytes 262176 | tf_op jit(solution)/shard_map/all_to_all | solution.py:451
  78.2 5.7 %predict_part.1 = f32[8,8,16,128]{3,2,1,0:T(8,128)S(1)} custom-call(bf16[16,64,128]{2,1,0:T(8,128)(2,1)S(1)} %all-to-all-done.1.gather_ref, bf16[8,128,512]{2,1,0:T(8,128)(2,1)S(1)} %near_rows.1.near_ref), custom_call_target="tpu_custom_call" | custom-call | tf_op jit(solution)/shard_map/predict_part/pallas_call | solution.py:382
  83.9 23.8 %all_to_all.15 = f32[64,16,128]{2,1,0:T(8,128)S(1)} all-to-all(f32[64,16,128]{2,1,0:T(8,128)S(1)} %bitcast.19), channel_id=1, replica_groups=mesh['line'=8,'cable'=8,'gx'=4,'core'=2] {'line','gx','core'}, dimensions={0} | all-to-all | bytes 1048576 | tf_op jit(solution)/shard_map/all_to_all | solution.py:459
  107.7 1.0 finish_sum.1
  (8 shorter events, 0.1 us)
Async XLA Ops:
  0.6 19.4 %copy-start.3 = (s32[4,16]{1,0:T(4,128)S(1)}, s32[4,16]{1,0:T(4,128)}, u32[]{:S(2)}) copy-start(s32[4,16]{1,0:T(4,128)} %param.8) | copy-start | bytes 772
  0.7 19.6 %copy-start.1 = (bf16[4,16,512]{2,1,0:T(8,128)(2,1)S(1)}, bf16[4,16,512]{2,1,0:T(8,128)(2,1)}, u32[]{:S(2)}) copy-start(bf16[4,16,512]{2,1,0:T(8,128)(2,1)} %param.7) | copy-start | bytes 196612
  8.3 32.1 %copy-start = (s32[131072]{0:T(1024)S(1)}, s32[131072]{0:T(1024)}, u32[]{:S(2)}) copy-start(s32[131072]{0:T(1024)} %order_hbm.1) | copy-start | bytes 1572868
  8.3 41.1 %all-to-all-start = ((bf16[64,32,128]{2,1,0:T(8,128)(2,1)}), bf16[64,32,128]{2,1,0:T(8,128)(2,1)S(1)}, u32[]{:S(2)}, u32[]{:S(2)}) async-start(bf16[64,32,128]{2,1,0:T(8,128)(2,1)} %bitcast.23), calls=%async_computation | async-start | bytes 1048576 | tf_op jit(solution)/shard_map/all_to_all | solution.py:431
  21.4 12.9 %collective-permute-start = (bf16[1,144,256]{2,1,0:T(8,128)(2,1)S(1)}, bf16[1,144,256]{2,1,0:T(8,128)(2,1)S(1)}, u32[]{:S(2)}, u32[]{:S(2)}) collective-permute-start(bf16[1,144,256]{2,1,0:T(8,128)(2,1)S(1)} %maximum_bitcast_fusion), channel_id=1, source_target_pairs={{0,256},{64,320},{128,384},{192,448},{256,0},{320,64},{384,128},{4... | collective-permute-start | bytes 221192 | tf_op jit(solution)/shard_map/ppermute | solution.py:295
  34.3 12.7 %collective-permute-start.1 = (bf16[2,144,256]{2,1,0:T(8,128)(2,1)S(1)}, bf16[2,144,256]{2,1,0:T(8,128)(2,1)S(1)}, u32[]{:S(2)}, u32[]{:S(2)}) collective-permute-start(bf16[2,144,256]{2,1,0:T(8,128)(2,1)S(1)} %pad_maximum_fusion.2), channel_id=1, source_target_pairs={{0,128},{64,192},{128,0},{192,64},{256,384},{320,448},{384,256},{4... | collective-permute-start | bytes 442376 | tf_op jit(solution)/shard_map/ppermute | solution.py:295
  40.5 8.4 %copy-start.2 = (s32[128,16]{0,1:T(8,128)S(1)}, s32[128,16]{0,1:T(8,128)}, u32[]{:S(2)}) copy-start(s32[128,16]{0,1:T(8,128)} %param.9) | copy-start | bytes 24580
  47.0 10.0 %collective-permute-start.2 = (bf16[4,144,256]{2,1,0:T(8,128)(2,1)S(1)}, bf16[4,144,256]{2,1,0:T(8,128)(2,1)S(1)}, u32[]{:S(2)}, u32[]{:S(2)}) collective-permute-start(bf16[4,144,256]{2,1,0:T(8,128)(2,1)S(1)} %pad_maximum_fusion.1), channel_id=1, source_target_pairs={{0,64},{64,0},{128,192},{192,128},{256,320},{320,256},{384,448},{4... | collective-permute-start | bytes 884744 | tf_op jit(solution)/shard_map/ppermute | solution.py:295
  57.0 9.6 %collective-permute-start.3 = (bf16[8,144,256]{2,1,0:T(8,128)(2,1)S(1)}, bf16[8,144,256]{2,1,0:T(8,128)(2,1)S(1)}, u32[]{:S(2)}, u32[]{:S(2)}) collective-permute-start(bf16[8,144,256]{2,1,0:T(8,128)(2,1)S(1)} %pad_maximum_fusion.own_ref), channel_id=1, source_target_pairs={{0,1},{1,0},{2,3},{3,2},{4,5},{5,4},{6,7},{7,6},{8,9},{9,8},{10,11... | collective-permute-start | bytes 1769480 | tf_op jit(solution)/shard_map/ppermute | solution.py:295
  60.2 18.0 %all-to-all-start.1 = ((bf16[16,64,128]{2,1,0:T(8,128)(2,1)}), bf16[16,64,128]{2,1,0:T(8,128)(2,1)S(1)}, u32[]{:S(2)}, u32[]{:S(2)}) async-start(bf16[16,64,128]{2,1,0:T(8,128)(2,1)} %bitcast.8), calls=%async_computation.1 | async-start | bytes 524288 | tf_op jit(solution)/shard_map/all_to_all | solution.py:451

commit v3 on v2

--- a/solution.py
+++ b/solution.py
@@ -74,8 +74,8 @@
     lax.fori_loop(0, rows // MOVED, tile, 0)
 
 
-def send_kernel(where_ref, order_hbm, rec_hbm, out_ref, order_ref, rec_ref, source, code, sems):
-    line, me = where_ref[0], where_ref[1]
+def send_kernel(line_ref, me_ref, order_hbm, rec_hbm, out_ref, order_ref, rec_ref, source, code, sems):
+    line, me = line_ref[0], me_ref[0]
     order_copy = pltpu.make_async_copy(
         order_hbm.at[pl.ds(pl.multiple_of(me * PER_DEV, PER_DEV), PER_DEV)], order_ref, sems.at[0]
     )
@@ -116,11 +116,12 @@
     picked_rows(code, source, out_ref, lambda total, base: total)
 
 
-def send(recorded, trace_order, where):
+def send(recorded, trace_order, line, me):
     return pl.pallas_call(
         send_kernel,
         out_shape=jax.ShapeDtypeStruct((OWNERS * HALF, LANES), bf16),
         in_specs=[
+            pl.BlockSpec(memory_space=pltpu.SMEM),
             pl.BlockSpec(memory_space=pltpu.SMEM),
             pl.BlockSpec(memory_space=pltpu.HBM),
             pl.BlockSpec(memory_space=pltpu.HBM),
@@ -135,61 +136,69 @@
         ],
         compiler_params=params(58),
         name="send_rows",
-    )(where, trace_order, recorded)
-
-
-def place_kernel(me_ref, order_ref, out_ref, key, chip_ref, row_ref):
+    )(line, me, trace_order, recorded)
+
+
+def place_kernel(me_ref, order_ref, out_ref, held):
     me = me_ref[0]
     before = earlier_matrix()
     carry = jnp.zeros((OWNERS, 1), f32)
     for c in range(PER_DEV // TILE):
         lanes = slice(c * TILE, (c + 1) * TILE)
         order = order_ref[:, lanes]
-        mine = jnp.where(owner_of(order) == me, 1.0, 0.0).astype(f32)
-        count = jnp.dot(mine.astype(bf16), before, preferred_element_type=f32) + carry
-        carry = carry + jnp.sum(mine, axis=1, keepdims=True)
-        key[:, lanes] = jnp.where(mine > 0.5, count, -1.0)
+        mine = owner_of(order) == me
+        ones = jnp.where(mine, 1.0, 0.0).astype(f32)
+        count = jnp.dot(ones.astype(bf16), before, preferred_element_type=f32) + carry
+        carry = carry + jnp.sum(ones, axis=1, keepdims=True)
+        distance = iota((OWNERS, TILE), 1) + c * TILE - count.astype(i32)
         receiver = order & (REC_DEV - 1)
-        chip_ref[:, lanes] = (receiver & (SHARES - 1)).astype(f32)
-        row_ref[:, lanes] = ((receiver >> 4) * APT_DEV + ((order >> REC_BITS) & 15)).astype(f32)
+        share, rho = receiver & (SHARES - 1), receiver >> 4
+        code = share * 64 + (rho & (UPPER - 1)) * APT_DEV + ((order >> REC_BITS) & 15)
+        code = code + (rho >> 2) * 1024 + 1
+        held[:, lanes] = jnp.where(mine, code * PER_DEV + distance, 0)
+
+    lane = iota((8, LANES), 1)
+    row = iota((8, LANES), 0)
+    columns = PER_DEV // LANES
+    none = jnp.zeros((8, LANES), i32)
 
     def group(g, carry):
-        eight = pl.ds(pl.multiple_of(g * 8, 8), 8)
-        all_keys = key[eight, :]
-        chips = chip_ref[eight, :]
-        local_rows = row_ref[eight, :]
-        ones = jnp.ones((4, PER_DEV), f32)
-        want = iota((HALF, PER_DEV), 0)
-        for part in range(2):
-            four = slice(4 * part, 4 * part + 4)
-            values = jnp.concatenate([chips[four], local_rows[four], ones, 0 * ones], axis=0)
-            values = values.astype(bf16)
-            blocks = []
-            for half in range(2):
-                wanted = (want + half * HALF).astype(f32).astype(bf16)
-                for b in range(4):
-                    mine = all_keys[4 * part + b : 4 * part + b + 1].astype(bf16)
-                    blocks.append(jnp.where(wanted == mine, bf16(1), bf16(0)))
-            onehot = jnp.concatenate(blocks, axis=0)
-            found = lax.dot_general(
-                values, onehot, (((1,), (1,)), ((), ())), preferred_element_type=f32
-            )
-            own = (iota((16, TILE), 0) & 3) == ((iota((16, TILE), 1) & (LANES - 1)) >> 5)
-            found = jnp.where(own, found, 0.0)
-            chip = jnp.sum(found[0:4], axis=0, keepdims=True).astype(i32)
-            row = jnp.sum(found[4:8], axis=0, keepdims=True).astype(i32)
-            valid = jnp.sum(found[8:12], axis=0, keepdims=True) > 0.5
-            code = chip * 64 + (row & 63)
-            at = pl.ds(pl.multiple_of((2 * g + part) * LANES, LANES), LANES)
+        rows = pl.ds(pl.multiple_of(g * 8, 8), 8)
+        kept = [held[rows, c * LANES : (c + 1) * LANES] for c in range(columns)]
+        for bit in range(11):
+            step = 1 << bit
+            if step < LANES:
+                turned = [pltpu.roll(v, LANES - step, 1) for v in kept] + [none]
+                coming = [
+                    jnp.where(lane < LANES - step, turned[c], turned[c + 1])
+                    for c in range(columns)
+                ]
+            else:
+                skip = step // LANES
+                coming = kept[skip:] + [none] * skip
+            kept = [
+                jnp.where((new & step) != 0, new, jnp.where((old & step) != 0, 0, old))
+                for new, old in zip(coming, kept)
+            ]
+        slots = kept[0]
+        for half in range(2):
+            spread = none
+            for r in range(4):
+                shift = (32 * r - 32 * half) % LANES
+                turned = pltpu.roll(slots, shift, 1) if shift else slots
+                spread = jnp.where(((row & 3) == r) & ((lane >> 5) == r), turned, spread)
+            field = spread >> 11
             for upper in range(2):
-                placed = jnp.where(valid & ((row >> 6) == upper), code, -1)
-                for half in range(2):
-                    out_ref[2 * upper + half : 2 * upper + half + 1, at] = placed[
-                        :, half * LANES : (half + 1) * LANES
-                    ]
+                want = (field > 1024 * upper) & (field <= 1024 * upper + 1024)
+                value = jnp.where(want, field - 1024 * upper, 0).astype(f32)
+                for part in range(2):
+                    placed = jnp.sum(value[4 * part : 4 * part + 4], axis=0, keepdims=True)
+                    at = pl.ds(pl.multiple_of((2 * g + part) * LANES, LANES), LANES)
+                    v = 2 * upper + half
+                    out_ref[v : v + 1, at] = placed.astype(i32) - 1
         return carry
 
-    lax.fori_loop(0, OWNERS // 8, group, 0)
+    lax.fori_loop(0, OWNERS // 8, group, 0, unroll=4)
 
 
 def place(orders, me):
@@ -201,7 +210,7 @@
             pl.BlockSpec(memory_space=pltpu.VMEM),
         ],
         out_specs=pl.BlockSpec(memory_space=pltpu.VMEM),
-        scratch_shapes=[pltpu.VMEM((OWNERS, PER_DEV), f32)] * 3,
+        scratch_shapes=[pltpu.VMEM((OWNERS, PER_DEV), i32)],
         compiler_params=params(12),
         cost_estimate=pl.CostEstimate(
             flops=4 * 2**30, bytes_accessed=2**20, transcendentals=0
@@ -421,13 +430,13 @@
     me = lax.axis_index(("cable",) + gate).astype(i32)
     line = lax.axis_index("line").astype(i32)
 
-    shots = shot_traces.reshape(SHOT_DEV, APT_DEV, NT // TAP, TAP)
-    shots = jnp.transpose(shots, (2, 0, 1, 3)).reshape(NT // TAP * SHOT_DEV, APT_DEV * TAP)
-    picks = jnp.tile(jnp.repeat(line_picks, TAP, axis=1), (4, 1)).astype(bf16)
-    held = jnp.concatenate([shots, picks], axis=0)[None]
-    four = swapped(held, "line", 4)
-
-    outgoing = send(recorded, trace_order, jnp.stack([line, me]))
+    spare = ((0, 0), (0, 0), (0, LANES - 1))
+    joined = jnp.concatenate(
+        [shot_traces, jnp.pad(line_picks.astype(bf16)[:, :, None], spare)], axis=2
+    )
+    far = swapped(joined, "line", 4)
+
+    outgoing = send(recorded, trace_order, line.reshape(1), me.reshape(1))
     got = lax.all_to_all(
         outgoing.reshape(OWNERS, HALF, LANES),
         ("cable",) + gate,
@@ -435,10 +444,14 @@
         concat_axis=0,
         tiled=True,
     )
-    late, four, trace_order, aperture_mask = lax.optimization_barrier(
-        (outgoing, four, trace_order, aperture_mask)
-    )
-    held = jnp.concatenate([held, four], axis=0)
+    late, joined, far, trace_order, aperture_mask = lax.optimization_barrier(
+        (outgoing, joined, far, trace_order, aperture_mask)
+    )
+    both = jnp.stack([joined, far])
+    shots = both[:, :, :, :NT].reshape(2, SHOT_DEV, APT_DEV, NT // TAP, TAP)
+    shots = jnp.transpose(shots, (0, 3, 1, 2, 4)).reshape(2, NT // TAP * SHOT_DEV, APT_DEV * TAP)
+    picks = jnp.tile(jnp.repeat(both[:, :, :, NT], TAP, axis=2), (1, 4, 1))
+    held = jnp.concatenate([shots, picks], axis=1)
     two = swapped(held, "line", 2)
     keys = place(trace_order.reshape(OWNERS, PER_DEV), me.reshape(1))
     keys, two = lax.optimization_barrier((keys, two))

time: 109 us -> 106 us (0.972)
  Pallas kernels: 26.3 us -> 22 us
  local copies, waits for them, and re-layouts: 1.85 us -> 3.16 us
  starting transfers between devices: 39.9 us -> 38.6 us
    pallas_call x1, Pallas kernels: 5.9 us -> 2.33 us  [place(): pl.pallas_call(place_kernel, out_shape=jax.ShapeDtypeStruct((4, OWNERS *...]
  transfers between devices with their start and end apart: 6 -> 6, of which waited for: 4 -> 3; matrix products, arithmetic and copies ran while one was open for 2% -> 3% of each run, Pallas kernels for 11% -> 15%
where the time goes in v3:
time: 106 us; the launch traced here: 105 us
  starting transfers between devices  38.6 us (36%)
  blocking collectives  23.6 us (22%)
  Pallas kernels  22 us (21%)
  waiting for transfers between devices  16 us (15%)
  local copies, waits for them, and re-layouts  3.16 us (3%)
  other arithmetic  1.81 us (2%)
    all_to_all x1, blocking collectives, on_device(): lax.all_to_all(part.reshape(OWNERS, 4 * UPPER, LANES), ('line',) + gate,...  23.6 us
    ppermute x4, starting transfers between devices, swapped(): return lax.ppermute(held, axis, [(i, i ^ bit) for i in range(size)])  22 us
    all_to_all x1, starting transfers between devices, on_device(): lax.all_to_all(outgoing.reshape(OWNERS, HALF, LANES), ('cable',) + gate,...  11.1 us
    all_to_all x1, waiting for transfers between devices, on_device(): lax.all_to_all(mine.reshape(SHARES, 64, LANES), ('line', 'core'), split_a...  10.9 us
    pallas_call x1, Pallas kernels, send(): pl.pallas_call(send_kernel, out_shape=jax.ShapeDtypeStruct((OWNERS * HALF...  6.81 us
    pallas_call x1, Pallas kernels, predict(): pl.pallas_call(predict_kernel, out_shape=jax.ShapeDtypeStruct((LINES, GAT...  5.67 us
    all_to_all x1, starting transfers between devices, on_device(): lax.all_to_all(mine.reshape(SHARES, 64, LANES), ('line', 'core'), split_a...  5.5 us
    pallas_call x1, Pallas kernels, receive(): pl.pallas_call(receive_kernel, out_shape=jax.ShapeDtypeStruct((SHARES * 6...  5.42 us
  transfers between devices with their start and end apart: 6, of which 3 were waited for; matrix products, arithmetic and copies ran while one was open for 3% of the time, Pallas kernels for 15%

profile of v3, /device:TPU:1, one launch (start us, length us, event | category | flops | bytes accessed | tf_op | source)
XLA Modules:
  0.0 105.4 jit_solution(6473755669755352787)
XLA Ops:
  0.0 0.7 convert_bitcast_fusion
  0.7 0.1 copy.12
  0.8 0.8 fusion.2
  1.7 11.5 %collective-permute-start = (bf16[4,16,640]{2,1,0:T(8,128)(2,1)S(1)}, bf16[4,16,640]{2,1,0:T(8,128)(2,1)S(1)}, u32[]{:S(2)}, u32[]{:S(2)}) collective-permute-start(bf16[4,16,640]{2,1,0:T(8,128)(2,1)S(1)} %fusion.2), channel_id=1, source_target_pairs={{0,256},{64,320},{128,384},{192,448},{256,0},{320,64},{384,128},{4... | collective-permute-start | bytes 245768 | tf_op jit(solution)/shard_map/ppermute | solution.py:304
  13.1 6.8 %send_rows.1 = bf16[2048,128]{1,0:T(8,128)(2,1)} custom-call(s32[1]{0:T(128)} %bitcast.1.line_ref, s32[1]{0:T(128)} %bitcast.me_ref, s32[131072]{0:T(1024)} %order_hbm.1, bf16[2048,512]{1,0:T(8,128)(2,1)} %rec_hbm.1), custom_call_target="tpu_custom_call" | custom-call | tf_op jit(solution)/shard_map/send_rows/pallas_call | solution.py:120
  19.9 11.1 %all-to-all-start = ((bf16[64,32,128]{2,1,0:T(8,128)(2,1)}), bf16[64,32,128]{2,1,0:T(8,128)(2,1)S(1)}, u32[]{:S(2)}, u32[]{:S(2)}) async-start(bf16[64,32,128]{2,1,0:T(8,128)(2,1)} %bitcast.29), calls=%async_computation | async-start | bytes 1048576 | tf_op jit(solution)/shard_map/all_to_all | solution.py:440
  31.0 0.0 collective-permute-done
  31.1 0.1 fusion.3
  31.2 0.8 reshape.47
  32.0 0.0 copy-start
  32.0 0.4 copy.9
  32.4 1.0 reshape.48
  33.4 0.1 broadcast_in_dim.10
  33.5 0.1 tile.10
  33.7 4.0 %collective-permute-start.1 = (bf16[2,144,256]{2,1,0:T(8,128)(2,1)S(1)}, bf16[2,144,256]{2,1,0:T(8,128)(2,1)S(1)}, u32[]{:S(2)}, u32[]{:S(2)}) collective-permute-start(bf16[2,144,256]{2,1,0:T(8,128)(2,1)S(1)} %constant_dynamic-update-slice_fusion), channel_id=1, source_target_pairs={{0,128},{64,192},{128,0},{192,64},{256,384},{320,448},{384,256},{4... | collective-permute-start | bytes 442376 | tf_op jit(solution)/shard_map/ppermute | solution.py:304
  37.7 0.0 copy-done
  37.7 0.1 reshape.46.order_ref
  37.8 0.0 copy-start.1
  37.8 2.3 %place_rows.1.key_ref = s32[4,2048]{1,0:T(4,128)S(1)} custom-call(s32[1]{0:T(128)} %bitcast.me_ref, s32[64,2048]{1,0:T(8,128)S(1)} %reshape.46.order_ref), custom_call_target="tpu_custom_call" | custom-call | flops 4294967296 | bytes 1048576 | tf_op jit(solution)/shard_map/place_rows/pallas_call | solution.py:205
  40.1 4.5 %collective-permute-done.1 = bf16[2,144,256]{2,1,0:T(8,128)(2,1)S(1)} collective-permute-done((bf16[2,144,256]{2,1,0:T(8,128)(2,1)S(1)}, bf16[2,144,256]{2,1,0:T(8,128)(2,1)S(1)}, u32[]{:S(2)}, u32[]{:S(2)}) %collective-permute-start.1) | collective-permute-done | bytes 147488 | tf_op jit(solution)/shard_map/ppermute | solution.py:304
  44.6 2.9 %collective-permute-start.2 = (bf16[4,144,256]{2,1,0:T(8,128)(2,1)S(1)}, bf16[4,144,256]{2,1,0:T(8,128)(2,1)S(1)}, u32[]{:S(2)}, u32[]{:S(2)}) collective-permute-start(bf16[4,144,256]{2,1,0:T(8,128)(2,1)S(1)} %pad_maximum_fusion.1), channel_id=1, source_target_pairs={{0,64},{64,0},{128,192},{192,128},{256,320},{320,256},{384,448},{4... | collective-permute-start | bytes 884744 | tf_op jit(solution)/shard_map/ppermute | solution.py:304
  47.5 0.0 copy-done.1
  47.6 0.1 reshape.51
  47.7 0.1 copy.10
  47.8 0.1 reshape.52
  47.9 0.2 copy.11.mask_ref
  48.1 0.7 all-to-all-done
  48.8 5.4 %receive_rows.1 = bf16[1024,128]{1,0:T(8,128)(2,1)} custom-call(s32[4,2048]{1,0:T(4,128)S(1)} %place_rows.1.key_ref, bf16[2048,128]{1,0:T(8,128)(2,1)S(1)} %bitcast.26, bf16[1024,128]{1,0:T(8,128)(2,1)S(1)} %copy.11.mask_ref), custom_call_target="tpu_custom_call" | custom-call | tf_op jit(solution)/shard_map/receive_rows/pallas_call | solution.py:246
  54.2 0.0 collective-permute-done.2
  54.2 0.1 pad_maximum_fusion.own_ref
  54.2 3.7 %collective-permute-start.3 = (bf16[8,144,256]{2,1,0:T(8,128)(2,1)S(1)}, bf16[8,144,256]{2,1,0:T(8,128)(2,1)S(1)}, u32[]{:S(2)}, u32[]{:S(2)}) collective-permute-start(bf16[8,144,256]{2,1,0:T(8,128)(2,1)S(1)} %pad_maximum_fusion.own_ref), channel_id=1, source_target_pairs={{0,1},{1,0},{2,3},{3,2},{4,5},{5,4},{6,7},{7,6},{8,9},{9,8},{10,11... | collective-permute-start | bytes 1769480 | tf_op jit(solution)/shard_map/ppermute | solution.py:304
  57.9 5.5 %all-to-all-start.1 = ((bf16[16,64,128]{2,1,0:T(8,128)(2,1)}), bf16[16,64,128]{2,1,0:T(8,128)(2,1)S(1)}, u32[]{:S(2)}, u32[]{:S(2)}) async-start(bf16[16,64,128]{2,1,0:T(8,128)(2,1)} %bitcast.10), calls=%async_computation.1 | async-start | bytes 524288 | tf_op jit(solution)/shard_map/all_to_all | solution.py:464
  63.4 0.1 pad_add_fusion.where_ref
  63.5 0.0 collective-permute-done.3.other_ref
  63.5 0.8 near_rows.1.near_ref
  64.3 10.9 %all-to-all-done.1.gather_ref = bf16[16,64,128]{2,1,0:T(8,128)(2,1)S(1)} async-done(((bf16[16,64,128]{2,1,0:T(8,128)(2,1)}), bf16[16,64,128]{2,1,0:T(8,128)(2,1)S(1)}, u32[]{:S(2)}, u32[]{:S(2)}) %all-to-all-start.1) | async-done | bytes 262176 | tf_op jit(solution)/shard_map/all_to_all | solution.py:464
  75.1 5.7 %predict_part.1 = f32[8,8,16,128]{3,2,1,0:T(8,128)S(1)} custom-call(bf16[16,64,128]{2,1,0:T(8,128)(2,1)S(1)} %all-to-all-done.1.gather_ref, bf16[8,128,512]{2,1,0:T(8,128)(2,1)S(1)} %near_rows.1.near_ref), custom_call_target="tpu_custom_call" | custom-call | tf_op jit(solution)/shard_map/predict_part/pallas_call | solution.py:391
  80.8 23.6 %all_to_all.15 = f32[64,16,128]{2,1,0:T(8,128)S(1)} all-to-all(f32[64,16,128]{2,1,0:T(8,128)S(1)} %bitcast.25), channel_id=1, replica_groups=mesh['line'=8,'cable'=8,'gx'=4,'core'=2] {'line','gx','core'}, dimensions={0} | all-to-all | bytes 1048576 | tf_op jit(solution)/shard_map/all_to_all | solution.py:472
  104.4 1.0 finish_sum.1
  (8 shorter events, 0.1 us)
Async XLA Ops:
  1.7 29.4 %collective-permute-start = (bf16[4,16,640]{2,1,0:T(8,128)(2,1)S(1)}, bf16[4,16,640]{2,1,0:T(8,128)(2,1)S(1)}, u32[]{:S(2)}, u32[]{:S(2)}) collective-permute-start(bf16[4,16,640]{2,1,0:T(8,128)(2,1)S(1)} %fusion.2), channel_id=1, source_target_pairs={{0,256},{64,320},{128,384},{192,448},{256,0},{320,64},{384,128},{4... | collective-permute-start | bytes 245768 | tf_op jit(solution)/shard_map/ppermute | solution.py:304
  19.9 28.8 %all-to-all-start = ((bf16[64,32,128]{2,1,0:T(8,128)(2,1)}), bf16[64,32,128]{2,1,0:T(8,128)(2,1)S(1)}, u32[]{:S(2)}, u32[]{:S(2)}) async-start(bf16[64,32,128]{2,1,0:T(8,128)(2,1)} %bitcast.29), calls=%async_computation | async-start | bytes 1048576 | tf_op jit(solution)/shard_map/all_to_all | solution.py:440
  32.0 5.7 %copy-start = (s32[131072]{0:T(1024)S(1)}, s32[131072]{0:T(1024)}, u32[]{:S(2)}) copy-start(s32[131072]{0:T(1024)} %order_hbm.1) | copy-start | bytes 1572868
  33.7 10.9 %collective-permute-start.1 = (bf16[2,144,256]{2,1,0:T(8,128)(2,1)S(1)}, bf16[2,144,256]{2,1,0:T(8,128)(2,1)S(1)}, u32[]{:S(2)}, u32[]{:S(2)}) collective-permute-start(bf16[2,144,256]{2,1,0:T(8,128)(2,1)S(1)} %constant_dynamic-update-slice_fusion), channel_id=1, source_target_pairs={{0,128},{64,192},{128,0},{192,64},{256,384},{320,448},{384,256},{4... | collective-permute-start | bytes 442376 | tf_op jit(solution)/shard_map/ppermute | solution.py:304
  37.8 9.7 %copy-start.1 = (s32[128,16]{0,1:T(8,128)S(1)}, s32[128,16]{0,1:T(8,128)}, u32[]{:S(2)}) copy-start(s32[128,16]{0,1:T(8,128)} %param.9) | copy-start | bytes 24580
  44.6 9.5 %collective-permute-start.2 = (bf16[4,144,256]{2,1,0:T(8,128)(2,1)S(1)}, bf16[4,144,256]{2,1,0:T(8,128)(2,1)S(1)}, u32[]{:S(2)}, u32[]{:S(2)}) collective-permute-start(bf16[4,144,256]{2,1,0:T(8,128)(2,1)S(1)} %pad_maximum_fusion.1), channel_id=1, source_target_pairs={{0,64},{64,0},{128,192},{192,128},{256,320},{320,256},{384,448},{4... | collective-permute-start | bytes 884744 | tf_op jit(solution)/shard_map/ppermute | solution.py:304
  54.2 9.3 %collective-permute-start.3 = (bf16[8,144,256]{2,1,0:T(8,128)(2,1)S(1)}, bf16[8,144,256]{2,1,0:T(8,128)(2,1)S(1)}, u32[]{:S(2)}, u32[]{:S(2)}) collective-permute-start(bf16[8,144,256]{2,1,0:T(8,128)(2,1)S(1)} %pad_maximum_fusion.own_ref), channel_id=1, source_target_pairs={{0,1},{1,0},{2,3},{3,2},{4,5},{5,4},{6,7},{7,6},{8,9},{9,8},{10,11... | collective-permute-start | bytes 1769480 | tf_op jit(solution)/shard_map/ppermute | solution.py:304
  57.9 17.2 %all-to-all-start.1 = ((bf16[16,64,128]{2,1,0:T(8,128)(2,1)}), bf16[16,64,128]{2,1,0:T(8,128)(2,1)S(1)}, u32[]{:S(2)}, u32[]{:S(2)}) async-start(bf16[16,64,128]{2,1,0:T(8,128)(2,1)} %bitcast.10), calls=%async_computation.1 | async-start | bytes 524288 | tf_op jit(solution)/shard_map/all_to_all | solution.py:464

commit v4 on v3

--- a/solution.py
+++ b/solution.py
@@ -435,8 +435,9 @@
         [shot_traces, jnp.pad(line_picks.astype(bf16)[:, :, None], spare)], axis=2
     )
     far = swapped(joined, "line", 4)
-
-    outgoing = send(recorded, trace_order, line.reshape(1), me.reshape(1))
+    far, line_at = lax.optimization_barrier((far, line.reshape(1)))
+
+    outgoing = send(recorded, trace_order, line_at, me.reshape(1))
     got = lax.all_to_all(
         outgoing.reshape(OWNERS, HALF, LANES),
         ("cable",) + gate,
@@ -452,11 +453,8 @@
     shots = jnp.transpose(shots, (0, 3, 1, 2, 4)).reshape(2, NT // TAP * SHOT_DEV, APT_DEV * TAP)
     picks = jnp.tile(jnp.repeat(both[:, :, :, NT], TAP, axis=2), (1, 4, 1))
     held = jnp.concatenate([shots, picks], axis=1)
-    two = swapped(held, "line", 2)
+    near_by = [swapped(held, "line", bit) for bit in (2, 1, 3)]
     keys = place(trace_order.reshape(OWNERS, PER_DEV), me.reshape(1))
-    keys, two = lax.optimization_barrier((keys, two))
-    held = jnp.concatenate([held, two], axis=0)
-    one = swapped(held, "line", 1)
     weights = aperture_mask.astype(bf16).reshape(2, UPPER, SHARES, APT_DEV)
     weights = jnp.transpose(weights, (2, 1, 3, 0)).reshape(SHARES * 64, 2)
     weights = jnp.repeat(weights, WIDTH, axis=1)
@@ -464,8 +462,8 @@
     gathers = lax.all_to_all(
         mine.reshape(SHARES, 64, LANES), ("line", "core"), split_axis=0, concat_axis=0, tiled=True
     )
-    late, one = lax.optimization_barrier((mine, one))
-    own = jnp.concatenate([held, one], axis=0)
+    late, near_by = lax.optimization_barrier((mine, near_by))
+    own = jnp.concatenate([held] + near_by, axis=0)
     other = swapped(own, "core", 1)
     near_all = near(jnp.stack([line, lax.axis_index("core").astype(i32)]), own, other)
     part = predict(gathers, near_all)

time: 106 us -> 110 us (1.038)
  starting transfers between devices: 38.6 us -> 43.6 us
    ppermute x4 -> x5, waiting for transfers between devices: 4.47 us -> 1.91 us  [swapped(): return lax.ppermute(held, axis, [(i, i ^ bit) for i in range(size)])]
    all_to_all x1, starting transfers between devices: 5.5 us -> 7.8 us  [on_device(): lax.all_to_all(mine.reshape(SHARES, 64, LANES), ('line', 'core'), split_a...]
    all_to_all x1, waiting for transfers between devices: 0.67 us -> 2.8 us  [on_device(): lax.all_to_all(outgoing.reshape(OWNERS, HALF, LANES), ('cable',) + gate,...]
    all_to_all x1, starting transfers between devices: 11.1 us -> 12.8 us  [on_device(): lax.all_to_all(outgoing.reshape(OWNERS, HALF, LANES), ('cable',) + gate,...]
    ppermute x4 -> x5, starting transfers between devices: 22 us -> 23 us  [swapped(): return lax.ppermute(held, axis, [(i, i ^ bit) for i in range(size)])]
  transfers between devices with their start and end apart: 6 -> 7, of which waited for: 3 -> 3; matrix products, arithmetic and copies ran while one was open for 3% -> 3% of each run, Pallas kernels for 15% -> 8%
where the time goes in v4:
time: 110 us
  starting transfers between devices  43.6 us (40%)
  blocking collectives  23.3 us (21%)
  Pallas kernels  22 us (20%)
  waiting for transfers between devices  15.6 us (14%)
  local copies, waits for them, and re-layouts  3.16 us (3%)
  other arithmetic  1.8 us (2%)
    all_to_all x1, blocking collectives, on_device(): lax.all_to_all(part.reshape(OWNERS, 4 * UPPER, LANES), ('line',) + gate,...  23.3 us
    ppermute x5, starting transfers between devices, swapped(): return lax.ppermute(held, axis, [(i, i ^ bit) for i in range(size)])  23 us
    all_to_all x1, starting transfers between devices, on_device(): lax.all_to_all(outgoing.reshape(OWNERS, HALF, LANES), ('cable',) + gate,...  12.8 us
    all_to_all x1, waiting for transfers between devices, on_device(): lax.all_to_all(mine.reshape(SHARES, 64, LANES), ('line', 'core'), split_a...  10.9 us
    all_to_all x1, starting transfers between devices, on_device(): lax.all_to_all(mine.reshape(SHARES, 64, LANES), ('line', 'core'), split_a...  7.8 us
    pallas_call x1, Pallas kernels, send(): pl.pallas_call(send_kernel, out_shape=jax.ShapeDtypeStruct((OWNERS * HALF...  6.82 us
    pallas_call x1, Pallas kernels, predict(): pl.pallas_call(predict_kernel, out_shape=jax.ShapeDtypeStruct((LINES, GAT...  5.66 us
    pallas_call x1, Pallas kernels, receive(): pl.pallas_call(receive_kernel, out_shape=jax.ShapeDtypeStruct((SHARES * 6...  5.42 us
  transfers between devices with their start and end apart: 7, of which 3 were waited for; matrix products, arithmetic and copies ran while one was open for 3% of the time, Pallas kernels for 8%

profile of v4, /device:TPU:1, one launch (start us, length us, event | category | flops | bytes accessed | tf_op | source)
XLA Modules:
  0.0 109.7 jit_solution(2863782416107246950)
XLA Ops:
  0.0 0.7 convert_bitcast_fusion
  0.7 0.1 copy.12
  0.8 0.8 fusion.2
  1.7 11.5 %collective-permute-start = (bf16[4,16,640]{2,1,0:T(8,128)(2,1)S(1)}, bf16[4,16,640]{2,1,0:T(8,128)(2,1)S(1)}, u32[]{:S(2)}, u32[]{:S(2)}) collective-permute-start(bf16[4,16,640]{2,1,0:T(8,128)(2,1)S(1)} %fusion.2), channel_id=1, source_target_pairs={{0,256},{64,320},{128,384},{192,448},{256,0},{320,64},{384,128},{4... | collective-permute-start | bytes 245768 | tf_op jit(solution)/shard_map/ppermute | solution.py:304
  13.1 1.9 %collective-permute-done = bf16[4,16,640]{2,1,0:T(8,128)(2,1)S(1)} collective-permute-done((bf16[4,16,640]{2,1,0:T(8,128)(2,1)S(1)}, bf16[4,16,640]{2,1,0:T(8,128)(2,1)S(1)}, u32[]{:S(2)}, u32[]{:S(2)}) %collective-permute-start) | collective-permute-done | bytes 81952 | tf_op jit(solution)/shard_map/ppermute | solution.py:304
  15.0 6.8 %send_rows.1 = bf16[2048,128]{1,0:T(8,128)(2,1)} custom-call(s32[1]{0:T(128)} %bitcast.2.line_ref, s32[1]{0:T(128)} %bitcast.me_ref, s32[131072]{0:T(1024)} %order_hbm.1, bf16[2048,512]{1,0:T(8,128)(2,1)} %rec_hbm.1), custom_call_target="tpu_custom_call" | custom-call | tf_op jit(solution)/shard_map/send_rows/pallas_call | solution.py:120
  21.8 12.8 %all-to-all-start = ((bf16[64,32,128]{2,1,0:T(8,128)(2,1)}), bf16[64,32,128]{2,1,0:T(8,128)(2,1)S(1)}, u32[]{:S(2)}, u32[]{:S(2)}) async-start(bf16[64,32,128]{2,1,0:T(8,128)(2,1)} %bitcast.29), calls=%async_computation | async-start | bytes 1048576 | tf_op jit(solution)/shard_map/all_to_all | solution.py:441
  34.7 0.1 fusion.3
  34.8 0.1 broadcast_in_dim.11
  34.9 0.1 tile.10
  35.0 0.0 copy-start
  35.0 0.8 reshape.53
  35.9 0.4 copy.11
  36.3 1.0 reshape.54
  37.3 3.7 %collective-permute-start.3 = (bf16[2,144,256]{2,1,0:T(8,128)(2,1)S(1)}, bf16[2,144,256]{2,1,0:T(8,128)(2,1)S(1)}, u32[]{:S(2)}, u32[]{:S(2)}) collective-permute-start(bf16[2,144,256]{2,1,0:T(8,128)(2,1)S(1)} %constant_dynamic-update-slice_fusion), channel_id=1, source_target_pairs={{0,192},{64,128},{128,64},{192,0},{256,448},{320,384},{384,320},{4... | collective-permute-start | bytes 442376 | tf_op jit(solution)/shard_map/ppermute | solution.py:304
  41.0 3.1 %collective-permute-start.2 = (bf16[2,144,256]{2,1,0:T(8,128)(2,1)S(1)}, bf16[2,144,256]{2,1,0:T(8,128)(2,1)S(1)}, u32[]{:S(2)}, u32[]{:S(2)}) collective-permute-start(bf16[2,144,256]{2,1,0:T(8,128)(2,1)S(1)} %constant_dynamic-update-slice_fusion), channel_id=1, source_target_pairs={{0,64},{64,0},{128,192},{192,128},{256,320},{320,256},{384,448},{4... | collective-permute-start | bytes 442376 | tf_op jit(solution)/shard_map/ppermute | solution.py:304
  44.2 2.4 %collective-permute-start.1 = (bf16[2,144,256]{2,1,0:T(8,128)(2,1)S(1)}, bf16[2,144,256]{2,1,0:T(8,128)(2,1)S(1)}, u32[]{:S(2)}, u32[]{:S(2)}) collective-permute-start(bf16[2,144,256]{2,1,0:T(8,128)(2,1)S(1)} %constant_dynamic-update-slice_fusion), channel_id=1, source_target_pairs={{0,128},{64,192},{128,0},{192,64},{256,384},{320,448},{384,256},{4... | collective-permute-start | bytes 442376 | tf_op jit(solution)/shard_map/ppermute | solution.py:304
  46.6 0.0 copy-done
  46.6 0.1 reshape.46.order_ref
  46.7 0.0 copy-start.1
  46.7 2.3 %place_rows.1.key_ref = s32[4,2048]{1,0:T(4,128)S(1)} custom-call(s32[1]{0:T(128)} %bitcast.me_ref, s32[64,2048]{1,0:T(8,128)S(1)} %reshape.46.order_ref), custom_call_target="tpu_custom_call" | custom-call | flops 4294967296 | bytes 1048576 | tf_op jit(solution)/shard_map/place_rows/pallas_call | solution.py:205
  49.0 0.0 copy-done.1
  49.1 0.1 reshape.49
  49.2 0.1 copy.9
  49.3 0.1 reshape.50
  49.4 0.2 copy.10.mask_ref
  49.6 2.8 %all-to-all-done = bf16[64,32,128]{2,1,0:T(8,128)(2,1)S(1)} async-done(((bf16[64,32,128]{2,1,0:T(8,128)(2,1)}), bf16[64,32,128]{2,1,0:T(8,128)(2,1)S(1)}, u32[]{:S(2)}, u32[]{:S(2)}) %all-to-all-start) | async-done | bytes 524320 | tf_op jit(solution)/shard_map/all_to_all | solution.py:441
  52.4 5.4 %receive_rows.1 = bf16[1024,128]{1,0:T(8,128)(2,1)} custom-call(s32[4,2048]{1,0:T(4,128)S(1)} %place_rows.1.key_ref, bf16[2048,128]{1,0:T(8,128)(2,1)S(1)} %bitcast.26, bf16[1024,128]{1,0:T(8,128)(2,1)S(1)} %copy.10.mask_ref), custom_call_target="tpu_custom_call" | custom-call | tf_op jit(solution)/shard_map/receive_rows/pallas_call | solution.py:246
  57.8 0.0 collective-permute-done.3
  57.8 0.0 collective-permute-done.2
  57.8 0.0 collective-permute-done.1
  57.8 0.1 pad_maximum_fusion.own_ref
  57.9 2.3 %collective-permute-start.4 = (bf16[8,144,256]{2,1,0:T(8,128)(2,1)S(1)}, bf16[8,144,256]{2,1,0:T(8,128)(2,1)S(1)}, u32[]{:S(2)}, u32[]{:S(2)}) collective-permute-start(bf16[8,144,256]{2,1,0:T(8,128)(2,1)S(1)} %pad_maximum_fusion.own_ref), channel_id=1, source_target_pairs={{0,1},{1,0},{2,3},{3,2},{4,5},{5,4},{6,7},{7,6},{8,9},{9,8},{10,11... | collective-permute-start | bytes 1769480 | tf_op jit(solution)/shard_map/ppermute | solution.py:304
  60.2 7.8 %all-to-all-start.1 = ((bf16[16,64,128]{2,1,0:T(8,128)(2,1)}), bf16[16,64,128]{2,1,0:T(8,128)(2,1)S(1)}, u32[]{:S(2)}, u32[]{:S(2)}) async-start(bf16[16,64,128]{2,1,0:T(8,128)(2,1)} %bitcast.7), calls=%async_computation.1 | async-start | bytes 524288 | tf_op jit(solution)/shard_map/all_to_all | solution.py:462
  68.0 0.1 pad_add_fusion.where_ref
  68.1 0.0 collective-permute-done.4.other_ref
  68.1 0.8 near_rows.1.near_ref
  68.9 10.9 %all-to-all-done.1.gather_ref = bf16[16,64,128]{2,1,0:T(8,128)(2,1)S(1)} async-done(((bf16[16,64,128]{2,1,0:T(8,128)(2,1)}), bf16[16,64,128]{2,1,0:T(8,128)(2,1)S(1)}, u32[]{:S(2)}, u32[]{:S(2)}) %all-to-all-start.1) | async-done | bytes 262176 | tf_op jit(solution)/shard_map/all_to_all | solution.py:462
  79.7 5.7 %predict_part.1 = f32[8,8,16,128]{3,2,1,0:T(8,128)S(1)} custom-call(bf16[16,64,128]{2,1,0:T(8,128)(2,1)S(1)} %all-to-all-done.1.gather_ref, bf16[8,128,512]{2,1,0:T(8,128)(2,1)S(1)} %near_rows.1.near_ref), custom_call_target="tpu_custom_call" | custom-call | tf_op jit(solution)/shard_map/predict_part/pallas_call | solution.py:391
  85.4 23.3 %all_to_all.15 = f32[64,16,128]{2,1,0:T(8,128)S(1)} all-to-all(f32[64,16,128]{2,1,0:T(8,128)S(1)} %bitcast.25), channel_id=1, replica_groups=mesh['line'=8,'cable'=8,'gx'=4,'core'=2] {'line','gx','core'}, dimensions={0} | all-to-all | bytes 1048576 | tf_op jit(solution)/shard_map/all_to_all | solution.py:470
  108.7 1.0 finish_sum.1
  (7 shorter events, 0.1 us)
Async XLA Ops:
  1.7 13.4 %collective-permute-start = (bf16[4,16,640]{2,1,0:T(8,128)(2,1)S(1)}, bf16[4,16,640]{2,1,0:T(8,128)(2,1)S(1)}, u32[]{:S(2)}, u32[]{:S(2)}) collective-permute-start(bf16[4,16,640]{2,1,0:T(8,128)(2,1)S(1)} %fusion.2), channel_id=1, source_target_pairs={{0,256},{64,320},{128,384},{192,448},{256,0},{320,64},{384,128},{4... | collective-permute-start | bytes 245768 | tf_op jit(solution)/shard_map/ppermute | solution.py:304
  21.8 30.5 %all-to-all-start = ((bf16[64,32,128]{2,1,0:T(8,128)(2,1)}), bf16[64,32,128]{2,1,0:T(8,128)(2,1)S(1)}, u32[]{:S(2)}, u32[]{:S(2)}) async-start(bf16[64,32,128]{2,1,0:T(8,128)(2,1)} %bitcast.29), calls=%async_computation | async-start | bytes 1048576 | tf_op jit(solution)/shard_map/all_to_all | solution.py:441
  35.0 11.6 %copy-start = (s32[131072]{0:T(1024)S(1)}, s32[131072]{0:T(1024)}, u32[]{:S(2)}) copy-start(s32[131072]{0:T(1024)} %order_hbm.1) | copy-start | bytes 1572868
  37.3 20.5 %collective-permute-start.3 = (bf16[2,144,256]{2,1,0:T(8,128)(2,1)S(1)}, bf16[2,144,256]{2,1,0:T(8,128)(2,1)S(1)}, u32[]{:S(2)}, u32[]{:S(2)}) collective-permute-start(bf16[2,144,256]{2,1,0:T(8,128)(2,1)S(1)} %constant_dynamic-update-slice_fusion), channel_id=1, source_target_pairs={{0,192},{64,128},{128,64},{192,0},{256,448},{320,384},{384,320},{4... | collective-permute-start | bytes 442376 | tf_op jit(solution)/shard_map/ppermute | solution.py:304
  41.0 16.8 %collective-permute-start.2 = (bf16[2,144,256]{2,1,0:T(8,128)(2,1)S(1)}, bf16[2,144,256]{2,1,0:T(8,128)(2,1)S(1)}, u32[]{:S(2)}, u32[]{:S(2)}) collective-permute-start(bf16[2,144,256]{2,1,0:T(8,128)(2,1)S(1)} %constant_dynamic-update-slice_fusion), channel_id=1, source_target_pairs={{0,64},{64,0},{128,192},{192,128},{256,320},{320,256},{384,448},{4... | collective-permute-start | bytes 442376 | tf_op jit(solution)/shard_map/ppermute | solution.py:304
  44.2 13.7 %collective-permute-start.1 = (bf16[2,144,256]{2,1,0:T(8,128)(2,1)S(1)}, bf16[2,144,256]{2,1,0:T(8,128)(2,1)S(1)}, u32[]{:S(2)}, u32[]{:S(2)}) collective-permute-start(bf16[2,144,256]{2,1,0:T(8,128)(2,1)S(1)} %constant_dynamic-update-slice_fusion), channel_id=1, source_target_pairs={{0,128},{64,192},{128,0},{192,64},{256,384},{320,448},{384,256},{4... | collective-permute-start | bytes 442376 | tf_op jit(solution)/shard_map/ppermute | solution.py:304
  46.7 2.4 %copy-start.1 = (s32[128,16]{0,1:T(8,128)S(1)}, s32[128,16]{0,1:T(8,128)}, u32[]{:S(2)}) copy-start(s32[128,16]{0,1:T(8,128)} %param.9) | copy-start | bytes 24580
  57.9 10.2 %collective-permute-start.4 = (bf16[8,144,256]{2,1,0:T(8,128)(2,1)S(1)}, bf16[8,144,256]{2,1,0:T(8,128)(2,1)S(1)}, u32[]{:S(2)}, u32[]{:S(2)}) collective-permute-start(bf16[8,144,256]{2,1,0:T(8,128)(2,1)S(1)} %pad_maximum_fusion.own_ref), channel_id=1, source_target_pairs={{0,1},{1,0},{2,3},{3,2},{4,5},{5,4},{6,7},{7,6},{8,9},{9,8},{10,11... | collective-permute-start | bytes 1769480 | tf_op jit(solution)/shard_map/ppermute | solution.py:304
  60.2 19.5 %all-to-all-start.1 = ((bf16[16,64,128]{2,1,0:T(8,128)(2,1)}), bf16[16,64,128]{2,1,0:T(8,128)(2,1)S(1)}, u32[]{:S(2)}, u32[]{:S(2)}) async-start(bf16[16,64,128]{2,1,0:T(8,128)(2,1)} %bitcast.7), calls=%async_computation.1 | async-start | bytes 524288 | tf_op jit(solution)/shard_map/all_to_all | solution.py:462
